TPU v7x, 32 devices: a whole 2x2x4 slice. The times are simulated.
32 devices in a mesh: grp: 2 (over x), blk: 16 (over z, y, core).
Axes of the slice: x: 2, y: 2, z: 4, core: 2. Of those that a mesh axis runs over, the one named last changes fastest.
Arguments:
- edge_state: bfloat16 [12288, 512], P(('grp', 'blk')), may hold values from -6 to 6
- basis: bfloat16 [768, 16, 16], P(('grp', 'blk')), may hold values from -1.5 to 1.5
- weights: bfloat16 [3, 512, 512], replicated, may hold values from -0.25 to 0.25
- partner: int32 [96], P(('grp', 'blk')), may hold values from 0 to 5, as said below
- cotangent: bfloat16 [12288, 512], P(('grp', 'blk')), may hold values from -6 to 6
Outputs:
- edge_out: bfloat16 [12288, 512], P(('grp', 'blk'))
- grad_state: bfloat16 [12288, 512], P(('grp', 'blk'))
- weight_grad: float32 [1536, 512], P(('grp', 'blk'))
Inputs may be any that keep to these rules, and one draw needn't show every extreme that they name: partner pairs the blocks of each group: partner[partner[k]] = k within the group, and a block may be its own partner. A device pairs at most 1 of its blocks with blocks of any one other device of its group, and exactly 1 with those of one of them.
All inputs are finite; a program needn't handle non-finite values.
Results may differ from a plain program's by a relative error of at most 0.008.
Values may be sent and summed in bfloat16 or wider, within the bound.
A program may use at most 64 MiB of HBM per device.

v0:
```python
import math

import jax
import jax.numpy as jnp
from jax import lax
from jax.sharding import PartitionSpec as P

NBR = 16
CAP = 1


def norm_rows(hidden):
    return hidden * lax.rsqrt(jnp.mean(hidden * hidden, axis=-1, keepdims=True) + 1e-06)


def layer_forward(hidden, weight):
    normed = norm_rows(hidden).astype(jnp.bfloat16)
    preact = jnp.dot(normed, weight, preferred_element_type=jnp.float32)
    return (hidden + jax.nn.silu(preact), normed, preact)


def layer_backward(hidden, normed, preact, weight, upstream):
    sigma = jax.nn.sigmoid(preact)
    grad_pre = (upstream * sigma * (1.0 + preact * (1.0 - sigma))).astype(jnp.bfloat16)
    grad_weight = lax.dot_general(
        normed, grad_pre, (((0,), (0,)), ((), ())), preferred_element_type=jnp.float32
    )
    grad_normed = lax.dot_general(
        grad_pre, weight, (((1,), (1,)), ((), ())), preferred_element_type=jnp.float32
    )
    inverse = lax.rsqrt(jnp.mean(hidden * hidden, axis=-1, keepdims=True) + 1e-06)
    unit = hidden * inverse
    inner = jnp.mean(grad_normed * unit, axis=-1, keepdims=True)
    return (upstream + inverse * (grad_normed - unit * inner), grad_weight)


def flip_rows(blocks):
    count, height, width = blocks.shape
    return blocks.reshape(count, height // 2, 2, width)[:, :, ::-1, :].reshape(count, height, width)


def route_plan(partner, own_index, group_count):
    block_count = partner.shape[0]
    target = partner // block_count
    remote = partner % block_count
    order = jnp.arange(block_count)
    same = target[:, None] == target[None, :]
    send_rank = jnp.sum(same & (order[None, :] < order[:, None]), axis=1)
    recv_rank = jnp.sum(same & (remote[None, :] < remote[:, None]), axis=1)
    local_pair = target == own_index
    slots = jnp.arange(group_count * CAP)
    send_slot = target * CAP + send_rank
    recv_slot = target * CAP + recv_rank
    pack_matrix = ((slots[:, None] == send_slot[None, :]) & ~local_pair[None, :]).astype(
        jnp.bfloat16
    )
    unpack_matrix = ((recv_slot[:, None] == slots[None, :]) & ~local_pair[:, None]).astype(
        jnp.bfloat16
    )
    return (pack_matrix, unpack_matrix, local_pair)


def pack_blocks(values, pack_matrix, block_count):
    blocks = values.reshape(block_count, -1, values.shape[1])
    return jnp.einsum("sn,nrd->srd", pack_matrix, blocks, preferred_element_type=jnp.bfloat16)


def unpack_blocks(arrived, unpack_matrix, local_pair, values, block_count):
    blocks = values.reshape(block_count, -1, values.shape[1])
    distant = jnp.einsum("ns,srd->nrd", unpack_matrix, arrived, preferred_element_type=jnp.bfloat16)
    joined = jnp.where(local_pair[:, None, None], blocks, distant)
    return flip_rows(joined).reshape(values.shape)


def local(edge_state, basis, weights, partner, cotangent):
    row_count, width = edge_state.shape
    block_count = partner.shape[0]
    group_count = lax.axis_size("grp")
    own_index = lax.axis_index("grp")
    total_edges = row_count * group_count * lax.axis_size("blk")
    pack_matrix, unpack_matrix, local_pair = route_plan(partner, own_index, group_count)
    mixed = jnp.einsum(
        "aij,ajd->aid",
        basis,
        edge_state.reshape(-1, NBR, width),
        preferred_element_type=jnp.float32,
    ).reshape(row_count, width)
    first, normed_one, pre_one = layer_forward(mixed, weights[0])
    second, normed_two, pre_two = layer_forward(first, weights[1])
    sent = second.astype(jnp.bfloat16)
    arrived = lax.all_to_all(
        pack_blocks(sent, pack_matrix, block_count), "grp", split_axis=0, concat_axis=0, tiled=True
    )
    reversed_state = unpack_blocks(arrived, unpack_matrix, local_pair, sent, block_count)
    summed = second + reversed_state.astype(jnp.float32)
    final, normed_three, pre_three = layer_forward(summed, weights[2])
    edge_out = final.astype(jnp.bfloat16)
    grad_summed, grad_three = layer_backward(
        summed, normed_three, pre_three, weights[2], cotangent.astype(jnp.float32)
    )
    grad_reversed = grad_summed.astype(jnp.bfloat16)
    returned = lax.all_to_all(
        pack_blocks(grad_reversed, pack_matrix, block_count),
        "grp",
        split_axis=0,
        concat_axis=0,
        tiled=True,
    )
    grad_sent = unpack_blocks(returned, unpack_matrix, local_pair, grad_reversed, block_count)
    grad_second = grad_summed + grad_sent.astype(jnp.float32)
    grad_first, grad_two = layer_backward(first, normed_two, pre_two, weights[1], grad_second)
    grad_mixed, grad_one = layer_backward(mixed, normed_one, pre_one, weights[0], grad_first)
    grad_round = grad_mixed.astype(jnp.bfloat16).reshape(-1, NBR, width)
    grad_state = (
        jnp.einsum("aij,aid->ajd", basis, grad_round, preferred_element_type=jnp.float32)
        .reshape(row_count, width)
        .astype(jnp.bfloat16)
    )
    local_grads = jnp.concatenate([grad_one, grad_two, grad_three], axis=0)
    group_part = lax.psum_scatter(
        local_grads.astype(jnp.bfloat16), "grp", scatter_dimension=0, tiled=True
    ).astype(jnp.float32)
    summed_grads = lax.psum_scatter(group_part, "blk", scatter_dimension=0, tiled=True)
    weight_grad = summed_grads * (1.0 / math.sqrt(total_edges))
    return (edge_out, grad_state, weight_grad)


def solution(mesh):
    in_specs = (
        P(("grp", "blk"), None),
        P(("grp", "blk"), None, None),
        P(),
        P(("grp", "blk")),
        P(("grp", "blk"), None),
    )
    out_specs = (P(("grp", "blk"), None), P(("grp", "blk"), None), P(("grp", "blk"), None))
    return jax.shard_map(local, mesh=mesh, in_specs=in_specs, out_specs=out_specs, check_vma=False)
```

profile of v0, /device:TPU:0, one launch (start us, length us, event | category | flops | bytes accessed | tf_op | source)
XLA Modules:
  0.0 162.7 jit_solution(10775921283349740770)
XLA Ops:
  7.2 0.0 copy-start
  7.2 1.0 copy.43
  8.2 0.0 copy-done
  8.2 0.0 copy-start.7
  8.3 0.4 multiply_reduce_fusion.5
  8.7 0.1 multiply_convert_fusion.2
  8.8 0.1 copy-done.7
  8.9 2.4 %multiply_reduce_fusion.4 = (f32[384]{0:T(512)S(1)}, f32[384,512]{1,0:T(8,128)S(1)}, f32[384,512]{1,0:T(8,128)}) fusion(f32[24,16,512]{2,1,0:T(8,128)S(1)} %get-tuple-element.22, bf16[384,512]{1,0:T(8,128)(2,1)S(1)} %bitcast.74, bf16[3,512,512]{2,1,0:T(8,128)(2,1)} %param.7), kind=kOutput, calls=%fused_computation.25 | convolution fusion | flops 202702464 | bytes 3278336 | tf_op jit(solution)/shard_map/dot_general | solution.py:18
  11.3 0.0 copy-done.11
  11.4 0.0 copy-start.12
  11.4 0.0 copy-start.14
  11.4 1.6 fusion.28
  13.0 0.0 copy-start.1
  13.0 0.2 convert_reduce_fusion.1
  13.2 0.0 copy-start.15
  13.2 0.5 fusion.17
  13.7 0.7 copy.34
  14.4 4.2 %all-to-all-start = ((bf16[2,128,512]{2,1,0:T(8,128)(2,1)}), bf16[2,128,512]{2,1,0:T(8,128)(2,1)S(1)}, u32[]{:S(2)}, u32[]{:S(2)}) async-start(bf16[2,128,512]{2,1,0:T(8,128)(2,1)} %copy.34), calls=%async_computation | async-start | bytes 524288 | tf_op jit(solution)/shard_map/all_to_all | solution.py:91
  18.6 0.1 rsqrt.34
  18.7 5.8 %all-to-all-done = bf16[2,128,512]{2,1,0:T(8,128)(2,1)S(1)} async-done(((bf16[2,128,512]{2,1,0:T(8,128)(2,1)}), bf16[2,128,512]{2,1,0:T(8,128)(2,1)S(1)}, u32[]{:S(2)}, u32[]{:S(2)}) %all-to-all-start) | async-done | bytes 262176 | tf_op jit(solution)/shard_map/all_to_all | solution.py:91
  24.5 0.0 copy-done.14
  24.5 0.8 convolution_select_fusion.1
  25.4 0.3 copy.37
  25.7 3.6 %rev.6 = bf16[3,64,2,512]{3,2,1,0:T(2,128)(2,1)S(1)} reverse(bf16[3,64,2,512]{3,2,1,0:T(2,128)(2,1)S(1)} %copy.37), dimensions={2} | reverse | bytes 786432 | tf_op jit(solution)/shard_map/rev | solution.py:39
  29.3 1.0 reshape.104
  30.3 1.6 %multiply_reduce_fusion.3 = (f32[384]{0:T(512)S(1)}, f32[384,512]{1,0:T(8,128)S(1)}) fusion(f32[384,512]{1,0:T(8,128)} %reshape.104, f32[384,512]{1,0:T(8,128)S(1)} %get-tuple-element.15, f32[384,512]{1,0:T(8,128)S(1)} %get-tuple-element.25), kind=kLoop, calls=%fused_computation.22 | loop fusion | flops 1572480 | bytes 3147264 | tf_op jit(solution)/shard_map/reduce_sum | solution.py:13
  32.0 0.0 copy-done.3
  32.0 0.0 copy-done.5
  32.0 1.4 fusion.1
  33.4 0.5 multiply_reduce_fusion.2
  33.9 0.3 copy-done.6
  34.2 0.2 fusion.30
  34.4 0.0 copy-start.10
  34.4 0.7 copy-done.10
  35.2 0.5 fusion.15
  35.6 0.7 copy.39
  36.4 4.1 %all-to-all-start.1 = ((bf16[2,128,512]{2,1,0:T(8,128)(2,1)}), bf16[2,128,512]{2,1,0:T(8,128)(2,1)}, u32[]{:S(2)}, u32[]{:S(2)}) async-start(bf16[2,128,512]{2,1,0:T(8,128)(2,1)} %copy.39), calls=%async_computation.1 | async-start | bytes 524288 | tf_op jit(solution)/shard_map/all_to_all | solution.py:102
  40.5 0.0 reduce-scatter.3.cloned.1.call-start
  40.5 2.4 %convolution_convert_fusion = bf16[512,512]{1,0:T(8,128)(2,1)} fusion(bf16[384,512]{1,0:T(8,128)(2,1)} %copy-done.6, f32[384,512]{1,0:T(8,128)S(1)} %get-tuple-element.10, f32[384]{0:T(512)S(1)} %add_rsqrt_fusion.1), kind=kOutput, calls=%fused_computation.1 | convolution fusion | flops 201981952 | bytes 1705472 | tf_op jit(solution)/shard_map/dot_general | solution.py:25
  42.9 2.9 %all-to-all-done.1 = bf16[2,128,512]{2,1,0:T(8,128)(2,1)} async-done(((bf16[2,128,512]{2,1,0:T(8,128)(2,1)}), bf16[2,128,512]{2,1,0:T(8,128)(2,1)}, u32[]{:S(2)}, u32[]{:S(2)}) %all-to-all-start.1) | async-done | bytes 262176 | tf_op jit(solution)/shard_map/all_to_all | solution.py:102
  45.7 1.9 %convolution_select_fusion = bf16[3,128,512]{2,0,1:T(4,128)(2,1)S(1)} fusion(pred[3]{0:T(512)(128)(4,1)} %copy-done.14, bf16[3,128,512]{2,1,0:T(8,128)(2,1)} %bitcast.72, bf16[2,128,512]{2,1,0:T(8,128)(2,1)} %all-to-all-done.1, pred[3]{0:T(512)(128)(4,1)} %copy-done.12, s32[3]{0:T(128)} %copy-done.15), kind=kOutput, calls=%fused_computation.5 | convolution fusion | flops 983052 | bytes 1048594 | tf_op jit(solution)/shard_map/ns,srd->nrd/dot_general | solution.py:70
  47.7 1.1 copy.42
  48.8 5.4 %rev.7 = bf16[3,64,2,512]{3,2,1,0:T(2,128)(2,1)} reverse(bf16[3,64,2,512]{3,2,1,0:T(2,128)(2,1)} %copy.42), dimensions={2} | reverse | bytes 786432 | tf_op jit(solution)/shard_map/rev | solution.py:39
  54.2 2.0 %reshape.105 = f32[384,512]{1,0:T(8,128)} reshape(bf16[3,64,2,512]{3,2,1,0:T(2,128)(2,1)} %rev.7) | data formatting | bytes 1179648 | tf_op jit(solution)/shard_map/convert_element_type | solution.py:110
  56.2 3.2 %multiply_convert_fusion.1 = (bf16[384,512]{1,0:T(8,128)(2,1)S(1)}, f32[384,512]{1,0:T(8,128)S(1)}, bf16[384,512]{1,0:T(8,128)(2,1)}) fusion(f32[384,512]{1,0:T(8,128)} %copy-done.1, f32[384,512]{1,0:T(8,128)} %reshape.105, f32[384,512]{1,0:T(8,128)S(1)} %get-tuple-element.29, f32[384]{0:T(512)S(1)} %broadcast_multiply_fusion.3, ...), kind=kLoop, calls=%fused_computation.18 | loop fusion | flops 4325376 | bytes 5901312 | tf_op jit(solution)/shard_map/convert_element_type | solution.py:24
  59.4 0.0 copy-done.4
  59.4 0.5 multiply_reduce_fusion.1
  59.9 0.5 convolution_convert_fusion.1
  60.4 0.1 copy-done.9
  60.5 0.4 multiply_convert_fusion
  61.0 0.5 multiply_reduce_fusion
  61.5 0.2 fusion.2
  61.7 0.5 convolution_convert_fusion.2
  62.2 0.3 copy-done.2
  62.5 1.3 pad_maximum_fusion
  63.8 0.0 reduce-scatter.3.cloned.1.call-update
  63.8 0.0 copy-start.8
  63.8 0.0 reduce-scatter.5.cloned.1.call-start
  63.9 26.8 %reduce-scatter.3.cloned.1.call-done = bf16[768,512]{1,0:T(8,128)(2,1)} async-done(((bf16[1536,512]{1,0:T(8,128)(2,1)}), bf16[768,512]{1,0:T(8,128)(2,1)}) %reduce-scatter.3.cloned.1.call-update) | async-done | bytes 786448 | tf_op jit(solution)/shard_map/reduce_scatter | solution.py:120
  90.6 2.5 %convert_element_type.93 = f32[768,512]{1,0:T(8,128)} convert(bf16[768,512]{1,0:T(8,128)(2,1)} %reduce-scatter.3.cloned.1.call-done) | non-fusion elementwise | flops 393216 | bytes 2359296 | tf_op jit(solution)/shard_map/convert_element_type | solution.py:122
  93.2 0.0 reduce-scatter.5.cloned.1.call-update
  93.2 1.0 convolution_convert_fusion.3
  94.2 60.1 %reduce-scatter.5.cloned.1.call-done = f32[48,512]{1,0:T(8,128)} async-done(((f32[768,512]{1,0:T(8,128)}), f32[48,512]{1,0:T(8,128)}) %reduce-scatter.5.cloned.1.call-update) | async-done | bytes 98320 | tf_op jit(solution)/shard_map/reduce_scatter | solution.py:123
  154.3 1.5 broadcast_multiply_fusion
  (26 shorter events, 0.1 us)
Async XLA Ops:
  7.2 1.1 copy-start
  8.2 0.6 copy-start.7
  8.9 2.4 %copy-start.11 = (s32[3]{0:T(128)S(1)}, s32[3]{0:T(128)}, u32[]{:S(2)}) copy-start(s32[3]{0:T(128)} %param.8) | copy-start | bytes 40
  11.4 13.1 %copy-start.12 = (pred[3]{0:T(512)(128)(4,1)}, pred[3]{0:T(512)(128)(4,1)S(1)}, u32[]{:S(2)}) copy-start(pred[3]{0:T(512)(128)(4,1)S(1)} %get-tuple-element.11) | copy-start | bytes 13
  11.4 13.1 %copy-start.14 = (pred[3]{0:T(512)(128)(4,1)}, pred[3]{0:T(512)(128)(4,1)S(1)}, u32[]{:S(2)}) copy-start(pred[3]{0:T(512)(128)(4,1)S(1)} %get-tuple-element.12) | copy-start | bytes 13
  13.0 17.3 %copy-start.1 = (f32[384,512]{1,0:T(8,128)}, f32[384,512]{1,0:T(8,128)S(1)}, u32[]{:S(2)}) copy-start(f32[384,512]{1,0:T(8,128)S(1)} %get-tuple-element.25) | copy-start | bytes 2359300
  13.2 12.1 %copy-start.15 = (s32[3]{0:T(128)}, s32[3]{0:T(128)S(1)}, u32[]{:S(2)}) copy-start(s32[3]{0:T(128)S(1)} %get-tuple-element.19) | copy-start | bytes 40
  13.2 12.1 %copy-start.16 = (s32[3]{0:T(128)}, s32[3]{0:T(128)S(1)}, u32[]{:S(2)}) copy-start(s32[3]{0:T(128)S(1)} %get-tuple-element.20) | copy-start | bytes 40
  14.4 10.1 %all-to-all-start = ((bf16[2,128,512]{2,1,0:T(8,128)(2,1)}), bf16[2,128,512]{2,1,0:T(8,128)(2,1)S(1)}, u32[]{:S(2)}, u32[]{:S(2)}) async-start(bf16[2,128,512]{2,1,0:T(8,128)(2,1)} %copy.34), calls=%async_computation | async-start | bytes 524288 | tf_op jit(solution)/shard_map/all_to_all | solution.py:91
  30.3 1.7 %copy-start.3 = (bf16[3,512,512]{2,1,0:T(8,128)(2,1)S(1)}, bf16[3,512,512]{2,1,0:T(8,128)(2,1)}, u32[]{:S(2)}) copy-start(bf16[3,512,512]{2,1,0:T(8,128)(2,1)} %param.7) | copy-start | bytes 4718596
  30.3 1.7 %copy-start.5 = (bf16[384,512]{1,0:T(8,128)(2,1)S(1)}, bf16[384,512]{1,0:T(8,128)(2,1)}, u32[]{:S(2)}) copy-start(bf16[384,512]{1,0:T(8,128)(2,1)} %param.9) | copy-start | bytes 1179652
  33.4 0.7 copy-start.6
  34.2 1.0 copy-start.13
  34.2 1.0 copy-start.17
  34.4 0.7 copy-start.10
  36.4 9.4 %all-to-all-start.1 = ((bf16[2,128,512]{2,1,0:T(8,128)(2,1)}), bf16[2,128,512]{2,1,0:T(8,128)(2,1)}, u32[]{:S(2)}, u32[]{:S(2)}) async-start(bf16[2,128,512]{2,1,0:T(8,128)(2,1)} %copy.39), calls=%async_computation.1 | async-start | bytes 524288 | tf_op jit(solution)/shard_map/all_to_all | solution.py:102
  40.5 50.2 %reduce-scatter.3.cloned.1.call-start = ((), (), s32[]{:S(2)}) async-start(), calls=%async_computation.4 | async-start | bytes 2359296 | tf_op jit(solution)/shard_map/reduce_scatter | solution.py:120
  56.2 3.2 %copy-start.4 = (bf16[3,512,512]{2,1,0:T(8,128)(2,1)S(1)}, bf16[3,512,512]{2,1,0:T(8,128)(2,1)}, u32[]{:S(2)}) copy-start(bf16[3,512,512]{2,1,0:T(8,128)(2,1)} %param.7) | copy-start | bytes 4718596
  59.4 1.1 copy-start.9
  61.5 1.0 copy-start.2
  63.8 29.4 %copy-start.8 = (bf16[24,16,16]{1,2,0:T(8,128)(2,1)S(1)}, bf16[24,16,16]{1,2,0:T(8,128)(2,1)}, u32[]{:S(2)}) copy-start(bf16[24,16,16]{1,2,0:T(8,128)(2,1)} %copy-done.7) | copy-start | bytes 36868
  63.8 90.4 %reduce-scatter.5.cloned.1.call-start = ((), (), s32[]{:S(2)}) async-start(), calls=%async_computation.5 | async-start | bytes 1671168 | tf_op jit(solution)/shard_map/reduce_scatter | solution.py:123
Sparse Core Ops, SparseCore 0:
  63.9 26.6 reduce-scatter.2
  94.7 59.4 reduce-scatter.4
where the time goes:
time: 164 us; the launch traced here: 163 us
  waiting for transfers between devices  95.5 us (58%)
  local copies, waits for them, and re-layouts  17.6 us (11%)
  matrix products  15.3 us (9%)
  between operations  14.3 us (9%)
  other arithmetic  11.5 us (7%)
  starting transfers between devices  8.39 us (5%)
    reduce_scatter x1, waiting for transfers between devices, local(): lax.psum_scatter(group_part, 'blk', scatter_dimension=0, tiled=True)  60.1 us
    reduce_scatter x1, waiting for transfers between devices, local(): lax.psum_scatter(local_grads.astype(jnp.bfloat16), 'grp', scatter_dimensi...  26.8 us
    rev x2, local copies, waits for them, and re-layouts, flip_rows(): blocks.reshape(count, height // 2, 2, width)[:, :, ::-1, :]  9.02 us
    all_to_all x1, waiting for transfers between devices, local(): lax.all_to_all(pack_blocks(sent, pack_matrix, block_count), 'grp', split_...  5.79 us
    dot_general x3, matrix products, layer_forward(): preact = jnp.dot(normed, weight, preferred_element_type=jnp.float32)  5.42 us
    all_to_all x1, starting transfers between devices, local(): lax.all_to_all(pack_blocks(sent, pack_matrix, block_count), 'grp', split_...  4.21 us
    all_to_all x1, starting transfers between devices, local(): lax.all_to_all(pack_blocks(grad_reversed, pack_matrix, block_count), 'grp...  4.1 us
    convert_element_type x2, other arithmetic, layer_backward(): (upstream * sigma * (1.0 + preact * (1.0 - sigma))).astype(jnp.bfloat16)  3.65 us
  transfers between devices with their start and end apart: 4, of which 4 were waited for; matrix products, arithmetic and copies ran while one was open for 2% of the time, Pallas kernels for 0%

commit v1 on v0

--- a/solution.py
+++ b/solution.py
@@ -1,12 +1,374 @@
+import functools
 import math
 
 import jax
 import jax.numpy as jnp
 from jax import lax
+from jax.experimental import pallas as pl
+from jax.experimental.pallas import tpu as pltpu
 from jax.sharding import PartitionSpec as P
 
 NBR = 16
 CAP = 1
+BLOCK = 128
+CHUNK = 16
+EPS = 1e-06
+MESH = pl.DeviceIdType.MESH
+BF16 = jnp.bfloat16
+F32 = jnp.float32
+
+
+def dot(a, b, ca=1, cb=0):
+    return lax.dot_general(a, b, (((ca,), (cb,)), ((), ())), preferred_element_type=F32)
+
+
+def inverse_rms(h):
+    return lax.rsqrt(jnp.mean(h * h, axis=-1, keepdims=True) + EPS)
+
+
+def flip(x):
+    rows = x.shape[0]
+    even = lax.broadcasted_iota(jnp.int32, x.shape, 0) % 2 == 0
+    return jnp.where(even, pltpu.roll(x, rows - 1, 0), pltpu.roll(x, 1, 0))
+
+
+def mixing_matrix(basis):
+    rows = basis.shape[0]
+    spread = (
+        lax.broadcasted_iota(jnp.int32, (NBR, rows), 1) % NBR
+        == lax.broadcasted_iota(jnp.int32, (NBR, rows), 0)
+    ).astype(F32).astype(BF16)
+    wide = dot(basis, spread)
+    same = (
+        lax.broadcasted_iota(jnp.int32, (rows, rows), 0) // NBR
+        == lax.broadcasted_iota(jnp.int32, (rows, rows), 1) // NBR
+    )
+    return jnp.where(same, wide, 0.0).astype(BF16)
+
+
+def forward(h, w_ref, layer, n_ref, rows):
+    inv = inverse_rms(h)
+    normed = (h * inv).astype(BF16)
+    n_ref[layer, rows, :] = normed
+    pre = dot(normed, w_ref[layer])
+    s = 0.5 * jnp.tanh(0.5 * pre) + 0.5
+    slope = s * (1.0 + pre * (1.0 - s))
+    return h + pre * s, (inv, slope)
+
+
+def backward(h, saved, w_ref, layer, g, d_ref, rows):
+    inv, slope = saved
+    dpre = (g * slope).astype(BF16)
+    d_ref[layer, rows, :] = dpre
+    dn = dot(dpre, w_ref[layer], 1, 1)
+    u = h * inv
+    inner = jnp.mean(dn * u, axis=-1, keepdims=True)
+    return g + inv * (dn - u * inner)
+
+
+def kernel(
+    n_blk,
+    scale,
+    partner_ref,
+    state_ref,
+    basis_ref,
+    w_ref,
+    cot_ref,
+    out_ref,
+    gstate_ref,
+    wgrad_ref,
+    n_ref,
+    d_ref,
+    eout_ref,
+    gout_ref,
+    sent_ref,
+    give_ref,
+    take_ref,
+    half_ref,
+    own_ref,
+    half_in_ref,
+    part_ref,
+    part_in_ref,
+    piece_ref,
+    final_ref,
+    give_sem,
+    take_sem,
+    half_sem,
+    half_in_sem,
+    part_sem,
+    part_in_sem,
+    piece_sem,
+    final_sem,
+):
+    x = lax.axis_index("grp")
+    b = lax.axis_index("blk")
+    me = x * n_blk + b
+    core = b % 2
+    y = (b // 2) % 2
+    z = b // 4
+    count = 2 * n_blk
+    width = w_ref.shape[2]
+
+    barrier = pltpu.get_barrier_semaphore()
+
+    def greet(step, carry):
+        other = (me + step) % count
+        pl.semaphore_signal(
+            barrier, inc=1, device_id=(other // n_blk, other % n_blk), device_id_type=MESH
+        )
+        return carry
+
+    lax.fori_loop(1, count, greet, 0)
+
+    base = x * 3
+    p0, p1, p2 = partner_ref[0], partner_ref[1], partner_ref[2]
+    sides = [jnp.minimum(jnp.maximum(p - 2, 0), 1) - x for p in (p0, p1, p2)]
+    away0, away1, away2 = (side * side for side in sides)
+    first_pos = jnp.minimum(away1 + 2 * away2, 2)
+    pos1 = away0
+    pos2 = 2 - away2
+    shift = away0 * p1 + (1 - away0) * p0 - base - pos1
+    swapped = jnp.minimum(shift * shift, 1)
+    place = (1 - away0, jnp.minimum(away0 + 2 * away2, 2), 2 - 2 * away2)
+
+    def pair(ref):
+        return jnp.concatenate([ref[pos1], ref[pos2]], axis=0)
+
+    a_rows, b_rows = pl.ds(0, BLOCK), pl.ds(BLOCK, 2 * BLOCK)
+
+    def exchange(step):
+        return pltpu.make_async_remote_copy(
+            src_ref=give_ref.at[step],
+            dst_ref=take_ref.at[step],
+            send_sem=give_sem.at[step],
+            recv_sem=take_sem.at[step],
+            device_id=(1 - x, b),
+            device_id_type=MESH,
+        )
+
+    def local_reverse(v, step):
+        sent_ref[step] = v.astype(BF16).reshape(2, BLOCK, width)
+        other = jnp.concatenate(
+            [sent_ref[step, swapped], sent_ref[step, 1 - swapped]], axis=0
+        )
+        return flip(other.astype(F32))
+
+    def half_copy(layer):
+        return pltpu.make_async_remote_copy(
+            src_ref=half_ref.at[layer],
+            dst_ref=half_in_ref.at[layer],
+            send_sem=half_sem.at[layer],
+            recv_sem=half_in_sem.at[layer],
+            device_id=(x, b + 1 - 2 * core),
+            device_id_type=MESH,
+        )
+
+    half_rows = width // 2
+    quarter = half_rows // 4
+
+    def send_half(layer):
+        def columns(c):
+            return n_ref[layer, :, pl.ds(pl.multiple_of(c * half_rows, half_rows), half_rows)]
+
+        d = d_ref[layer]
+        half_ref[layer] = dot(columns(1 - core), d, 0, 0).astype(BF16)
+        half_copy(layer).start()
+        own_ref[layer] = dot(columns(core), d, 0, 0)
+
+    def part_copy(layer, r):
+        px = 1 - x if r >= 2 else x
+        py = 1 - y if r % 2 else y
+        return pltpu.make_async_remote_copy(
+            src_ref=part_ref.at[layer, 2 * px + py],
+            dst_ref=part_in_ref.at[layer, r - 1],
+            send_sem=part_sem.at[layer, r - 1],
+            recv_sem=part_in_sem.at[layer, r - 1],
+            device_id=(px, 4 * z + 2 * py + core),
+            device_id_type=MESH,
+        )
+
+    def send_parts(layer):
+        half_copy(layer).wait_recv()
+        total = own_ref[layer] + half_in_ref[layer].astype(F32)
+        part_ref[layer] = total.astype(BF16).reshape(4, quarter, width)
+        for r in (3, 2, 1):
+            part_copy(layer, r).start()
+
+    def piece_copy(layer, t):
+        c = 32 * layer + 16 * core + 4 * (2 * x + y) + t
+        dest = c // 3
+        copy = pltpu.make_async_remote_copy(
+            src_ref=piece_ref.at[layer, t],
+            dst_ref=final_ref.at[c % 3, z],
+            send_sem=piece_sem.at[layer, t],
+            recv_sem=final_sem.at[c % 3, z],
+            device_id=(dest // n_blk, dest % n_blk),
+            device_id_type=MESH,
+        )
+        return c, dest, copy
+
+    def send_pieces(layer):
+        for r in (1, 2, 3):
+            part_copy(layer, r).wait_recv()
+        total = part_ref[layer, 2 * x + y].astype(F32)
+        for r in (1, 2, 3):
+            total = total + part_in_ref[layer, r - 1].astype(F32)
+        piece_ref[layer] = total.astype(BF16).reshape(4, CHUNK, width)
+        for t in range(4):
+            c, dest, copy = piece_copy(layer, t)
+
+            @pl.when(dest != me)
+            def _():
+                copy.start()
+
+            @pl.when(dest == me)
+            def _():
+                final_ref[c % 3, z] = piece_ref[layer, t]
+
+    mix_a = mixing_matrix(basis_ref[first_pos])
+    mixed_a = dot(mix_a, state_ref[first_pos])
+    first_a, saved_a1 = forward(mixed_a, w_ref, 0, n_ref, a_rows)
+    second_a, saved_a2 = forward(first_a, w_ref, 1, n_ref, a_rows)
+    give_ref[0] = second_a.astype(BF16)
+    pl.semaphore_wait(barrier, count - 1)
+    exchange(0).start()
+
+    mix_b = mixing_matrix(pair(basis_ref))
+    mixed_b = dot(mix_b, pair(state_ref))
+    first_b, saved_b1 = forward(mixed_b, w_ref, 0, n_ref, b_rows)
+    second_b, saved_b2 = forward(first_b, w_ref, 1, n_ref, b_rows)
+    summed_b = second_b + local_reverse(second_b, 0)
+    final_b, saved_b3 = forward(summed_b, w_ref, 2, n_ref, b_rows)
+    eout_ref[pl.ds(1, 2)] = final_b.astype(BF16).reshape(2, BLOCK, width)
+    gs_b = backward(summed_b, saved_b3, w_ref, 2, pair(cot_ref).astype(F32), d_ref, b_rows)
+
+    exchange(0).wait_recv()
+    summed_a = second_a + flip(take_ref[0].astype(F32))
+    final_a, saved_a3 = forward(summed_a, w_ref, 2, n_ref, a_rows)
+    eout_ref[0] = final_a.astype(BF16)
+    gs_a = backward(
+        summed_a, saved_a3, w_ref, 2, cot_ref[first_pos].astype(F32), d_ref, a_rows
+    )
+    give_ref[1] = gs_a.astype(BF16)
+    exchange(1).start()
+
+    send_half(2)
+
+    gsec_b = gs_b + local_reverse(gs_b, 1)
+    gf_b = backward(first_b, saved_b2, w_ref, 1, gsec_b, d_ref, b_rows)
+    send_parts(2)
+    gm_b = backward(mixed_b, saved_b1, w_ref, 0, gf_b, d_ref, b_rows)
+    gout_ref[pl.ds(1, 2)] = dot(mix_b, gm_b.astype(BF16), 0, 0).astype(BF16).reshape(
+        2, BLOCK, width
+    )
+
+    exchange(1).wait_recv()
+    gsec_a = gs_a + flip(take_ref[1].astype(F32))
+    gf_a = backward(first_a, saved_a2, w_ref, 1, gsec_a, d_ref, a_rows)
+    send_half(1)
+    gm_a = backward(mixed_a, saved_a1, w_ref, 0, gf_a, d_ref, a_rows)
+    send_half(0)
+    send_parts(1)
+    send_pieces(2)
+    send_parts(0)
+    gout_ref[0] = dot(mix_a, gm_a.astype(BF16), 0, 0).astype(BF16)
+
+    for k in range(3):
+        out_ref[k] = eout_ref[place[k]]
+        gstate_ref[k] = gout_ref[place[k]]
+
+    send_pieces(1)
+    send_pieces(0)
+
+    for j in range(3):
+        c = 3 * me + j
+        i = c % 32
+        q = (i % 16) // 4
+        for plane in range(4):
+            source = (q // 2) * n_blk + 4 * plane + 2 * (q % 2) + i // 16
+
+            @pl.when(source != me)
+            def _():
+                pltpu.make_async_remote_copy(
+                    src_ref=piece_ref.at[0, 0],
+                    dst_ref=final_ref.at[j, plane],
+                    send_sem=piece_sem.at[0, 0],
+                    recv_sem=final_sem.at[j, plane],
+                    device_id=(1 - x, b),
+                    device_id_type=MESH,
+                ).wait_recv()
+
+    for j in range(3):
+        total = final_ref[j, 0].astype(F32)
+        for plane in range(1, 4):
+            total = total + final_ref[j, plane].astype(F32)
+        wgrad_ref[pl.ds(j * CHUNK, CHUNK), :] = total * scale
+
+    for step in range(2):
+        exchange(step).wait_send()
+    for layer in range(3):
+        half_copy(layer).wait_send()
+        for r in (1, 2, 3):
+            part_copy(layer, r).wait_send()
+        for t in range(4):
+            c, dest, copy = piece_copy(layer, t)
+
+            @pl.when(dest != me)
+            def _():
+                copy.wait_send()
+
+
+def local_fast(n_blk, edge_state, basis, weights, partner, cotangent):
+    rows, width = edge_state.shape
+    total_edges = rows * 2 * n_blk
+    half = width // 2
+    blocks = (rows // BLOCK, BLOCK, width)
+    vmem = pl.BlockSpec(memory_space=pltpu.VMEM)
+    dma = pltpu.SemaphoreType.DMA
+    out, gstate, wgrad = pl.pallas_call(
+        functools.partial(kernel, n_blk, 1.0 / math.sqrt(total_edges)),
+        out_shape=(
+            jax.ShapeDtypeStruct(blocks, BF16),
+            jax.ShapeDtypeStruct(blocks, BF16),
+            jax.ShapeDtypeStruct((3 * CHUNK, width), F32),
+        ),
+        in_specs=[pl.BlockSpec(memory_space=pltpu.SMEM)] + [vmem] * 4,
+        out_specs=(vmem, vmem, vmem),
+        scratch_shapes=[
+            pltpu.VMEM((3, rows, width), BF16),
+            pltpu.VMEM((3, rows, width), BF16),
+            pltpu.VMEM(blocks, BF16),
+            pltpu.VMEM(blocks, BF16),
+            pltpu.VMEM((2, 2, BLOCK, width), BF16),
+            pltpu.VMEM((2, BLOCK, width), BF16),
+            pltpu.VMEM((2, BLOCK, width), BF16),
+            pltpu.VMEM((3, half, width), BF16),
+            pltpu.VMEM((3, half, width), F32),
+            pltpu.VMEM((3, half, width), BF16),
+            pltpu.VMEM((3, 4, half // 4, width), BF16),
+            pltpu.VMEM((3, 3, half // 4, width), BF16),
+            pltpu.VMEM((3, 4, CHUNK, width), BF16),
+            pltpu.VMEM((3, 4, CHUNK, width), BF16),
+            dma((2,)),
+            dma((2,)),
+            dma((3,)),
+            dma((3,)),
+            dma((3, 3)),
+            dma((3, 3)),
+            dma((3, 4)),
+            dma((3, 4)),
+        ],
+        compiler_params=pltpu.CompilerParams(
+            collective_id=0, has_side_effects=True, vmem_limit_bytes=40 * 2**20
+        ),
+    )(
+        partner,
+        edge_state.reshape(blocks),
+        basis.reshape(-1, BLOCK, NBR),
+        weights,
+        cotangent.reshape(blocks),
+    )
+    return out.reshape(rows, width), gstate.reshape(rows, width), wgrad
 
 
 def norm_rows(hidden):
@@ -126,12 +488,12 @@
 
 
 def solution(mesh):
-    in_specs = (
-        P(("grp", "blk"), None),
-        P(("grp", "blk"), None, None),
-        P(),
-        P(("grp", "blk")),
-        P(("grp", "blk"), None),
-    )
-    out_specs = (P(("grp", "blk"), None), P(("grp", "blk"), None), P(("grp", "blk"), None))
-    return jax.shard_map(local, mesh=mesh, in_specs=in_specs, out_specs=out_specs, check_vma=False)
+    spread = P(("grp", "blk"))
+    wide = P(("grp", "blk"), None)
+    in_specs = (wide, P(("grp", "blk"), None, None), P(), spread, wide)
+    body = local
+    if mesh.shape["grp"] == 2 and mesh.shape["blk"] == 16:
+        body = functools.partial(local_fast, mesh.shape["blk"])
+    return jax.shard_map(
+        body, mesh=mesh, in_specs=in_specs, out_specs=(wide, wide, wide), check_vma=False
+    )

time: 164 us -> 42 us (0.26)
  the two profiles are of different devices: /device:TPU:0 before, /device:TPU:9 now
where the time goes in v1:
time: 42 us; the launch traced here: 41.7 us
  Pallas kernels  33.9 us (81%)
  local copies, waits for them, and re-layouts  7.16 us (17%)
  between operations  0.66 us (2%)
    pallas_call x1, Pallas kernels, local_fast(): pl.pallas_call(functools.partial(kernel, n_blk, 1.0 / math.sqrt(total_edg...  33.9 us
    unnamed x12, local copies, waits for them, and re-layouts  7.16 us

profile of v1, /device:TPU:9, one launch (start us, length us, event | category | flops | bytes accessed | tf_op | source)
XLA Modules:
  0.0 41.7 jit_solution(16626735806816426618)
XLA Ops:
  0.6 1.0 %copy.8 = bf16[24,16,16]{2,1,0:T(8,128)(2,1)S(1)} copy(bf16[24,16,16]{0,2,1:T(8,128)(2,1)} %param.6) | data formatting | bytes 24576 | tf_op args[1]
  1.6 0.0 copy-start
  1.6 1.4 %copy-done = bf16[3,512,512]{2,1,0:T(8,128)(2,1)S(1)} copy-done((bf16[3,512,512]{2,1,0:T(8,128)(2,1)S(1)}, bf16[3,512,512]{2,1,0:T(8,128)(2,1)}, u32[]{:S(2)}) %copy-start) | copy-done | bytes 1572888
  3.0 0.0 copy-start.1
  3.0 1.0 %copy-done.1 = bf16[384,512]{1,0:T(8,128)(2,1)S(1)} copy-done((bf16[384,512]{1,0:T(8,128)(2,1)S(1)}, bf16[384,512]{1,0:T(8,128)(2,1)}, u32[]{:S(2)}) %copy-start.1) | copy-done | bytes 393240
  4.0 0.0 copy-start.2
  4.0 1.0 %copy-done.2 = bf16[384,512]{1,0:T(8,128)(2,1)S(1)} copy-done((bf16[384,512]{1,0:T(8,128)(2,1)S(1)}, bf16[384,512]{1,0:T(8,128)(2,1)}, u32[]{:S(2)}) %copy-start.2) | copy-done | bytes 393240
  5.0 0.0 copy-start.3
  5.0 0.7 %copy-done.3 = s32[3]{0:T(128)S(1)} copy-done((s32[3]{0:T(128)S(1)}, s32[3]{0:T(128)}, u32[]{:S(2)}) %copy-start.3) | copy-done | bytes 36
  5.7 33.9 %shard_map.76 = (bf16[3,128,512]{2,1,0:T(8,128)(2,1)S(1)}, bf16[3,128,512]{2,1,0:T(8,128)(2,1)S(1)}, f32[48,512]{1,0:T(8,128)S(1)}) custom-call(s32[3]{0:T(128)S(1)} %copy-done.3, bf16[3,128,512]{2,1,0:T(8,128)(2,1)S(1)} %bitcast.7, bf16[3,128,16]{2,1,0:T(8,128)(2,1)S(1)} %bitcast.9, bf16[3,512,512]{2,1,0:T(8,128)(2,1)S(1)} %copy-done, ...), custom_call_target="tpu_custom_call" | custom-call | tf_op jit(solution)/shard_map/pallas_call | solution.py:328
  39.6 0.7 %copy.12 = bf16[384,512]{1,0:T(8,128)(2,1)} copy(bf16[384,512]{1,0:T(8,128)(2,1)S(1)} %bitcast.6) | data formatting | bytes 786432
  40.3 0.7 %copy.13 = bf16[384,512]{1,0:T(8,128)(2,1)} copy(bf16[384,512]{1,0:T(8,128)(2,1)S(1)} %bitcast.5) | data formatting | bytes 786432
  41.1 0.6 %copy.14 = f32[48,512]{1,0:T(8,128)} copy(f32[48,512]{1,0:T(8,128)S(1)} %get-tuple-element.14) | data formatting | bytes 196608
Async XLA Ops:
  1.6 1.4 %copy-start = (bf16[3,512,512]{2,1,0:T(8,128)(2,1)S(1)}, bf16[3,512,512]{2,1,0:T(8,128)(2,1)}, u32[]{:S(2)}) copy-start(bf16[3,512,512]{2,1,0:T(8,128)(2,1)} %w_ref.1) | copy-start | bytes 4718596
  3.0 1.0 %copy-start.1 = (bf16[384,512]{1,0:T(8,128)(2,1)S(1)}, bf16[384,512]{1,0:T(8,128)(2,1)}, u32[]{:S(2)}) copy-start(bf16[384,512]{1,0:T(8,128)(2,1)} %param.5) | copy-start | bytes 1179652
  4.0 1.0 %copy-start.2 = (bf16[384,512]{1,0:T(8,128)(2,1)S(1)}, bf16[384,512]{1,0:T(8,128)(2,1)}, u32[]{:S(2)}) copy-start(bf16[384,512]{1,0:T(8,128)(2,1)} %param.9) | copy-start | bytes 1179652
  5.0 0.7 %copy-start.3 = (s32[3]{0:T(128)S(1)}, s32[3]{0:T(128)}, u32[]{:S(2)}) copy-start(s32[3]{0:T(128)} %partner_ref.1) | copy-start | bytes 40

commit v2 on v1

--- a/solution.py
+++ b/solution.py
@@ -32,17 +32,29 @@
     return jnp.where(even, pltpu.roll(x, rows - 1, 0), pltpu.roll(x, 1, 0))
 
 
-def mixing_matrix(basis):
-    rows = basis.shape[0]
-    spread = (
-        lax.broadcasted_iota(jnp.int32, (NBR, rows), 1) % NBR
-        == lax.broadcasted_iota(jnp.int32, (NBR, rows), 0)
-    ).astype(F32).astype(BF16)
-    wide = dot(basis, spread)
-    same = (
-        lax.broadcasted_iota(jnp.int32, (rows, rows), 0) // NBR
-        == lax.broadcasted_iota(jnp.int32, (rows, rows), 1) // NBR
-    )
+def mixing_matrix(basis, blocks):
+    flat = basis.reshape(NBR * NBR, basis.shape[2])
+    rows = BLOCK * len(blocks)
+
+    def iota(shape, dim):
+        return lax.broadcasted_iota(jnp.int32, shape, dim)
+
+    def mask(hit):
+        return hit.astype(F32).astype(BF16)
+
+    atom_shape = (rows, basis.shape[2])
+    row = iota(atom_shape, 0)
+    first_atom = blocks[0] * (BLOCK // NBR)
+    if len(blocks) == 2:
+        first_atom = first_atom + (row // BLOCK) * ((blocks[1] - blocks[0]) * (BLOCK // NBR))
+    pick = mask(first_atom + (row % BLOCK) // NBR == iota(atom_shape, 1))
+    own = dot(pick, flat, 1, 1)
+    own_shape = (rows, NBR * NBR)
+    own = jnp.where(iota(own_shape, 0) % NBR == iota(own_shape, 1) // NBR, own, 0.0).astype(BF16)
+    spread_shape = (NBR * NBR, rows)
+    spread = mask(iota(spread_shape, 0) % NBR == iota(spread_shape, 1) % NBR)
+    wide = dot(own, spread)
+    same = iota((rows, rows), 0) // NBR == iota((rows, rows), 1) // NBR
     return jnp.where(same, wide, 0.0).astype(BF16)
 
 
@@ -69,14 +81,19 @@
 def kernel(
     n_blk,
     scale,
+    partner_hbm,
+    state_hbm,
+    basis_hbm,
+    w_hbm,
+    cot_hbm,
+    out_ref,
+    gstate_ref,
+    wgrad_ref,
     partner_ref,
     state_ref,
     basis_ref,
     w_ref,
     cot_ref,
-    out_ref,
-    gstate_ref,
-    wgrad_ref,
     n_ref,
     d_ref,
     eout_ref,
@@ -89,8 +106,11 @@
     half_in_ref,
     part_ref,
     part_in_ref,
+    quad_ref,
+    quad_in_ref,
     piece_ref,
     final_ref,
+    in_sem,
     give_sem,
     take_sem,
     half_sem,
@@ -109,6 +129,23 @@
     count = 2 * n_blk
     width = w_ref.shape[2]
 
+    loads = [
+        pltpu.make_async_copy(src, dst, in_sem.at[number])
+        for number, (src, dst) in enumerate(
+            [
+                (partner_hbm, partner_ref),
+                (basis_hbm, basis_ref),
+                (state_hbm, state_ref),
+                (w_hbm.at[0], w_ref.at[0]),
+                (w_hbm.at[1], w_ref.at[1]),
+                (w_hbm.at[2], w_ref.at[2]),
+                (cot_hbm, cot_ref),
+            ]
+        )
+    ]
+    for load in loads:
+        load.start()
+
     barrier = pltpu.get_barrier_semaphore()
 
     def greet(step, carry):
@@ -121,6 +158,7 @@
     lax.fori_loop(1, count, greet, 0)
 
     base = x * 3
+    loads[0].wait()
     p0, p1, p2 = partner_ref[0], partner_ref[1], partner_ref[2]
     sides = [jnp.minimum(jnp.maximum(p - 2, 0), 1) - x for p in (p0, p1, p2)]
     away0, away1, away2 = (side * side for side in sides)
@@ -164,7 +202,7 @@
         )
 
     half_rows = width // 2
-    quarter = half_rows // 4
+    eighth = half_rows // 8
 
     def send_half(layer):
         def columns(c):
@@ -175,27 +213,44 @@
         half_copy(layer).start()
         own_ref[layer] = dot(columns(core), d, 0, 0)
 
-    def part_copy(layer, r):
-        px = 1 - x if r >= 2 else x
-        py = 1 - y if r % 2 else y
+    def sides(layer, piece):
+        return (x, y) if piece == 1 and layer < 2 else (y, x)
+
+    def part_copy(layer, piece, hop):
+        along_x = (piece == 1 and layer < 2) == (hop == 0)
+        near, far = sides(layer, piece)
+        if hop == 0:
+            src, dst = part_ref.at[layer, piece, 1 - near], part_in_ref.at[layer, piece]
+        else:
+            src, dst = quad_ref.at[layer, piece, 1 - far], quad_in_ref.at[layer, piece]
         return pltpu.make_async_remote_copy(
-            src_ref=part_ref.at[layer, 2 * px + py],
-            dst_ref=part_in_ref.at[layer, r - 1],
-            send_sem=part_sem.at[layer, r - 1],
-            recv_sem=part_in_sem.at[layer, r - 1],
-            device_id=(px, 4 * z + 2 * py + core),
+            src_ref=src,
+            dst_ref=dst,
+            send_sem=part_sem.at[layer, piece, hop],
+            recv_sem=part_in_sem.at[layer, piece, hop],
+            device_id=(1 - x, b) if along_x else (x, b + 2 - 4 * y),
             device_id_type=MESH,
         )
 
     def send_parts(layer):
         half_copy(layer).wait_recv()
         total = own_ref[layer] + half_in_ref[layer].astype(F32)
-        part_ref[layer] = total.astype(BF16).reshape(4, quarter, width)
-        for r in (3, 2, 1):
-            part_copy(layer, r).start()
+        part_ref[layer] = total.astype(BF16).reshape(2, 2, 2, eighth, width)
+        for piece in range(2):
+            part_copy(layer, piece, 0).start()
+
+    def send_quads(layer):
+        for piece in range(2):
+            part_copy(layer, piece, 0).wait_recv()
+            near, _ = sides(layer, piece)
+            total = part_ref[layer, piece, near].astype(F32)
+            total = total + part_in_ref[layer, piece].astype(F32)
+            quad_ref[layer, piece] = total.astype(BF16)
+            part_copy(layer, piece, 1).start()
 
     def piece_copy(layer, t):
-        c = 32 * layer + 16 * core + 4 * (2 * x + y) + t
+        near, far = sides(layer, t // 2)
+        c = 32 * layer + 16 * core + 8 * (t // 2) + 4 * near + 2 * far + t % 2
         dest = c // 3
         copy = pltpu.make_async_remote_copy(
             src_ref=piece_ref.at[layer, t],
@@ -208,12 +263,12 @@
         return c, dest, copy
 
     def send_pieces(layer):
-        for r in (1, 2, 3):
-            part_copy(layer, r).wait_recv()
-        total = part_ref[layer, 2 * x + y].astype(F32)
-        for r in (1, 2, 3):
-            total = total + part_in_ref[layer, r - 1].astype(F32)
-        piece_ref[layer] = total.astype(BF16).reshape(4, CHUNK, width)
+        for piece in range(2):
+            part_copy(layer, piece, 1).wait_recv()
+            _, far = sides(layer, piece)
+            total = quad_ref[layer, piece, far].astype(F32)
+            total = total + quad_in_ref[layer, piece].astype(F32)
+            piece_ref[layer, pl.ds(2 * piece, 2)] = total.astype(BF16).reshape(2, CHUNK, width)
         for t in range(4):
             c, dest, copy = piece_copy(layer, t)
 
@@ -225,35 +280,40 @@
             def _():
                 final_ref[c % 3, z] = piece_ref[layer, t]
 
-    mix_a = mixing_matrix(basis_ref[first_pos])
+    loads[1].wait()
+    loads[2].wait()
+    mix_a = mixing_matrix(basis_ref[...], (first_pos,))
     mixed_a = dot(mix_a, state_ref[first_pos])
+    loads[3].wait()
     first_a, saved_a1 = forward(mixed_a, w_ref, 0, n_ref, a_rows)
+    loads[4].wait()
     second_a, saved_a2 = forward(first_a, w_ref, 1, n_ref, a_rows)
     give_ref[0] = second_a.astype(BF16)
     pl.semaphore_wait(barrier, count - 1)
     exchange(0).start()
 
-    mix_b = mixing_matrix(pair(basis_ref))
+    mix_b = mixing_matrix(basis_ref[...], (pos1, pos2))
     mixed_b = dot(mix_b, pair(state_ref))
     first_b, saved_b1 = forward(mixed_b, w_ref, 0, n_ref, b_rows)
     second_b, saved_b2 = forward(first_b, w_ref, 1, n_ref, b_rows)
     summed_b = second_b + local_reverse(second_b, 0)
+    loads[5].wait()
     final_b, saved_b3 = forward(summed_b, w_ref, 2, n_ref, b_rows)
     eout_ref[pl.ds(1, 2)] = final_b.astype(BF16).reshape(2, BLOCK, width)
-    gs_b = backward(summed_b, saved_b3, w_ref, 2, pair(cot_ref).astype(F32), d_ref, b_rows)
 
     exchange(0).wait_recv()
     summed_a = second_a + flip(take_ref[0].astype(F32))
     final_a, saved_a3 = forward(summed_a, w_ref, 2, n_ref, a_rows)
     eout_ref[0] = final_a.astype(BF16)
+    loads[6].wait()
     gs_a = backward(
         summed_a, saved_a3, w_ref, 2, cot_ref[first_pos].astype(F32), d_ref, a_rows
     )
     give_ref[1] = gs_a.astype(BF16)
     exchange(1).start()
 
+    gs_b = backward(summed_b, saved_b3, w_ref, 2, pair(cot_ref).astype(F32), d_ref, b_rows)
     send_half(2)
-
     gsec_b = gs_b + local_reverse(gs_b, 1)
     gf_b = backward(first_b, saved_b2, w_ref, 1, gsec_b, d_ref, b_rows)
     send_parts(2)
@@ -269,9 +329,12 @@
     gm_a = backward(mixed_a, saved_a1, w_ref, 0, gf_a, d_ref, a_rows)
     send_half(0)
     send_parts(1)
-    send_pieces(2)
+    send_quads(2)
     send_parts(0)
     gout_ref[0] = dot(mix_a, gm_a.astype(BF16), 0, 0).astype(BF16)
+    send_quads(1)
+    send_pieces(2)
+    send_quads(0)
 
     for k in range(3):
         out_ref[k] = eout_ref[place[k]]
@@ -283,9 +346,12 @@
     for j in range(3):
         c = 3 * me + j
         i = c % 32
-        q = (i % 16) // 4
+        near, far = (i // 4) % 2, (i // 2) % 2
+        x_first = ((i // 8) % 2) * (1 - c // 64)
+        from_y = near + x_first * (far - near)
+        from_x = far + x_first * (near - far)
         for plane in range(4):
-            source = (q // 2) * n_blk + 4 * plane + 2 * (q % 2) + i // 16
+            source = from_x * n_blk + 4 * plane + 2 * from_y + i // 16
 
             @pl.when(source != me)
             def _():
@@ -308,8 +374,9 @@
         exchange(step).wait_send()
     for layer in range(3):
         half_copy(layer).wait_send()
-        for r in (1, 2, 3):
-            part_copy(layer, r).wait_send()
+        for piece in range(2):
+            for hop in range(2):
+                part_copy(layer, piece, hop).wait_send()
         for t in range(4):
             c, dest, copy = piece_copy(layer, t)
 
@@ -332,9 +399,14 @@
             jax.ShapeDtypeStruct(blocks, BF16),
             jax.ShapeDtypeStruct((3 * CHUNK, width), F32),
         ),
-        in_specs=[pl.BlockSpec(memory_space=pltpu.SMEM)] + [vmem] * 4,
+        in_specs=[pl.BlockSpec(memory_space=pl.ANY)] * 5,
         out_specs=(vmem, vmem, vmem),
         scratch_shapes=[
+            pltpu.SMEM(partner.shape, jnp.int32),
+            pltpu.VMEM(blocks, BF16),
+            pltpu.VMEM((NBR, NBR, basis.shape[0]), BF16),
+            pltpu.VMEM(weights.shape, BF16),
+            pltpu.VMEM(blocks, BF16),
             pltpu.VMEM((3, rows, width), BF16),
             pltpu.VMEM((3, rows, width), BF16),
             pltpu.VMEM(blocks, BF16),
@@ -345,26 +417,29 @@
             pltpu.VMEM((3, half, width), BF16),
             pltpu.VMEM((3, half, width), F32),
             pltpu.VMEM((3, half, width), BF16),
-            pltpu.VMEM((3, 4, half // 4, width), BF16),
-            pltpu.VMEM((3, 3, half // 4, width), BF16),
+            pltpu.VMEM((3, 2, 2, 2, half // 8, width), BF16),
+            pltpu.VMEM((3, 2, 2, half // 8, width), BF16),
+            pltpu.VMEM((3, 2, 2, half // 8, width), BF16),
+            pltpu.VMEM((3, 2, half // 8, width), BF16),
             pltpu.VMEM((3, 4, CHUNK, width), BF16),
             pltpu.VMEM((3, 4, CHUNK, width), BF16),
+            dma((7,)),
             dma((2,)),
             dma((2,)),
             dma((3,)),
             dma((3,)),
-            dma((3, 3)),
-            dma((3, 3)),
+            dma((3, 2, 2)),
+            dma((3, 2, 2)),
             dma((3, 4)),
             dma((3, 4)),
         ],
         compiler_params=pltpu.CompilerParams(
-            collective_id=0, has_side_effects=True, vmem_limit_bytes=40 * 2**20
+            collective_id=0, has_side_effects=True, vmem_limit_bytes=56 * 2**20
         ),
     )(
         partner,
         edge_state.reshape(blocks),
-        basis.reshape(-1, BLOCK, NBR),
+        basis.transpose(1, 2, 0),
         weights,
         cotangent.reshape(blocks),
     )

time: 42 us -> 39.3 us (0.936)
  the two profiles are of different devices: /device:TPU:9 before, /device:TPU:0 now
where the time goes in v2:
time: 39.3 us; the launch traced here: 39.1 us
  Pallas kernels  34.3 us (87%)
  local copies, waits for them, and re-layouts  4.21 us (11%)
  between operations  0.65 us (2%)
    pallas_call x1, Pallas kernels, local_fast(): pl.pallas_call(functools.partial(kernel, n_blk, 1.0 / math.sqrt(total_edg...  34.3 us
    unnamed x5, local copies, waits for them, and re-layouts  4.21 us

profile of v2, /device:TPU:0, one launch (start us, length us, event | category | flops | bytes accessed | tf_op | source)
XLA Modules:
  0.0 39.1 jit_solution(1550834711519454358)
XLA Ops:
  0.6 34.3 %shard_map.76 = (bf16[3,128,512]{2,1,0:T(8,128)(2,1)}, bf16[3,128,512]{2,1,0:T(8,128)(2,1)}, f32[48,512]{1,0:T(8,128)}) custom-call(s32[3]{0:T(128)} %partner_hbm.1, bf16[3,128,512]{2,1,0:T(8,128)(2,1)} %bitcast.7, bf16[16,16,24]{2,1,0:T(8,128)(2,1)} %bitcast.9, bf16[3,512,512]{2,1,0:T(8,128)(2,1)} %w_hbm.1, bf16[3,128,512]{2,1,0:T(8,128)(2,1)} %bitcast.8), custom_call_target="tpu_custom_call" | custom-call | tf_op jit(solution)/shard_map/pallas_call | solution.py:395
  34.9 0.0 copy-start
  34.9 1.8 %copy.11 = bf16[384,512]{1,0:T(8,128)(2,1)} copy(bf16[384,512]{1,0:T(8,128)(2,1)} %bitcast.6) | data formatting | bytes 786432
  36.7 1.8 %copy.12 = bf16[384,512]{1,0:T(8,128)(2,1)} copy(bf16[384,512]{1,0:T(8,128)(2,1)} %bitcast.5) | data formatting | bytes 786432
  38.5 0.0 copy-done
  38.5 0.6 %copy.13 = f32[48,512]{1,0:T(8,128)} copy(f32[48,512]{1,0:T(8,128)S(1)} %copy-done) | data formatting | bytes 196608
Async XLA Ops:
  34.9 3.6 %copy-start = (f32[48,512]{1,0:T(8,128)S(1)}, f32[48,512]{1,0:T(8,128)}, u32[]{:S(2)}) copy-start(f32[48,512]{1,0:T(8,128)} %get-tuple-element.14) | copy-start | bytes 294916

commit v3 on v2

--- a/solution.py
+++ b/solution.py
@@ -80,7 +80,6 @@
 
 def kernel(
     n_blk,
-    scale,
     partner_hbm,
     state_hbm,
     basis_hbm,
@@ -109,6 +108,8 @@
     quad_ref,
     quad_in_ref,
     piece_ref,
+    piece_in_ref,
+    chunk_ref,
     final_ref,
     in_sem,
     give_sem,
@@ -118,6 +119,8 @@
     part_sem,
     part_in_sem,
     piece_sem,
+    piece_in_sem,
+    chunk_sem,
     final_sem,
 ):
     x = lax.axis_index("grp")
@@ -248,19 +251,16 @@
             quad_ref[layer, piece] = total.astype(BF16)
             part_copy(layer, piece, 1).start()
 
-    def piece_copy(layer, t):
-        near, far = sides(layer, t // 2)
-        c = 32 * layer + 16 * core + 8 * (t // 2) + 4 * near + 2 * far + t % 2
-        dest = c // 3
-        copy = pltpu.make_async_remote_copy(
-            src_ref=piece_ref.at[layer, t],
-            dst_ref=final_ref.at[c % 3, z],
-            send_sem=piece_sem.at[layer, t],
-            recv_sem=final_sem.at[c % 3, z],
-            device_id=(dest // n_blk, dest % n_blk),
+    def piece_copy(layer, hop):
+        plane = (z + hop) % 4
+        return pltpu.make_async_remote_copy(
+            src_ref=piece_ref.at[layer, plane],
+            dst_ref=piece_in_ref.at[layer, hop - 1],
+            send_sem=piece_sem.at[layer, hop - 1],
+            recv_sem=piece_in_sem.at[layer, hop - 1],
+            device_id=(x, (b + 4 * hop) % n_blk),
             device_id_type=MESH,
         )
-        return c, dest, copy
 
     def send_pieces(layer):
         for piece in range(2):
@@ -269,16 +269,41 @@
             total = quad_ref[layer, piece, far].astype(F32)
             total = total + quad_in_ref[layer, piece].astype(F32)
             piece_ref[layer, pl.ds(2 * piece, 2)] = total.astype(BF16).reshape(2, CHUNK, width)
-        for t in range(4):
-            c, dest, copy = piece_copy(layer, t)
-
-            @pl.when(dest != me)
-            def _():
-                copy.start()
-
-            @pl.when(dest == me)
-            def _():
-                final_ref[c % 3, z] = piece_ref[layer, t]
+        for hop in (2, 1, 3):
+            piece_copy(layer, hop).start()
+
+    def chunk_copy(layer):
+        piece = z // 2
+        x_first = piece if layer < 2 else 0
+        near = y + x_first * (x - y)
+        far = x + x_first * (y - x)
+        c = 32 * layer + 16 * core + 8 * piece + 4 * near + 2 * far + z % 2
+        dest = c // 3
+        copy = pltpu.make_async_remote_copy(
+            src_ref=chunk_ref.at[layer],
+            dst_ref=final_ref.at[c % 3],
+            send_sem=chunk_sem.at[layer],
+            recv_sem=final_sem.at[c % 3],
+            device_id=(dest // n_blk, dest % n_blk),
+            device_id_type=MESH,
+        )
+        return c, dest, copy
+
+    def send_chunk(layer):
+        total = piece_ref[layer, z].astype(F32)
+        for hop in (1, 2, 3):
+            piece_copy(layer, hop).wait_recv()
+            total = total + piece_in_ref[layer, hop - 1].astype(F32)
+        chunk_ref[layer] = total.astype(BF16)
+        c, dest, copy = chunk_copy(layer)
+
+        @pl.when(dest != me)
+        def _():
+            copy.start()
+
+        @pl.when(dest == me)
+        def _():
+            final_ref[c % 3] = chunk_ref[layer]
 
     loads[1].wait()
     loads[2].wait()
@@ -326,15 +351,16 @@
     gsec_a = gs_a + flip(take_ref[1].astype(F32))
     gf_a = backward(first_a, saved_a2, w_ref, 1, gsec_a, d_ref, a_rows)
     send_half(1)
+    send_quads(2)
     gm_a = backward(mixed_a, saved_a1, w_ref, 0, gf_a, d_ref, a_rows)
     send_half(0)
     send_parts(1)
-    send_quads(2)
+    send_pieces(2)
     send_parts(0)
     gout_ref[0] = dot(mix_a, gm_a.astype(BF16), 0, 0).astype(BF16)
     send_quads(1)
-    send_pieces(2)
     send_quads(0)
+    send_chunk(2)
 
     for k in range(3):
         out_ref[k] = eout_ref[place[k]]
@@ -342,33 +368,32 @@
 
     send_pieces(1)
     send_pieces(0)
+    send_chunk(1)
+    send_chunk(0)
 
     for j in range(3):
         c = 3 * me + j
         i = c % 32
+        layer = c // 32
+        piece = (i // 8) % 2
         near, far = (i // 4) % 2, (i // 2) % 2
-        x_first = ((i // 8) % 2) * (1 - c // 64)
+        x_first = piece * (1 - layer // 2)
         from_y = near + x_first * (far - near)
         from_x = far + x_first * (near - far)
-        for plane in range(4):
-            source = from_x * n_blk + 4 * plane + 2 * from_y + i // 16
-
-            @pl.when(source != me)
-            def _():
-                pltpu.make_async_remote_copy(
-                    src_ref=piece_ref.at[0, 0],
-                    dst_ref=final_ref.at[j, plane],
-                    send_sem=piece_sem.at[0, 0],
-                    recv_sem=final_sem.at[j, plane],
-                    device_id=(1 - x, b),
-                    device_id_type=MESH,
-                ).wait_recv()
-
-    for j in range(3):
-        total = final_ref[j, 0].astype(F32)
-        for plane in range(1, 4):
-            total = total + final_ref[j, plane].astype(F32)
-        wgrad_ref[pl.ds(j * CHUNK, CHUNK), :] = total * scale
+        source = from_x * n_blk + 4 * (2 * piece + i % 2) + 2 * from_y + i // 16
+
+        @pl.when(source != me)
+        def _():
+            pltpu.make_async_remote_copy(
+                src_ref=chunk_ref.at[0],
+                dst_ref=final_ref.at[j],
+                send_sem=chunk_sem.at[0],
+                recv_sem=final_sem.at[j],
+                device_id=(1 - x, b),
+                device_id_type=MESH,
+            ).wait_recv()
+
+        wgrad_ref[j] = final_ref[j]
 
     for step in range(2):
         exchange(step).wait_send()
@@ -377,12 +402,25 @@
         for piece in range(2):
             for hop in range(2):
                 part_copy(layer, piece, hop).wait_send()
-        for t in range(4):
-            c, dest, copy = piece_copy(layer, t)
-
-            @pl.when(dest != me)
-            def _():
-                copy.wait_send()
+        for hop in (1, 2, 3):
+            piece_copy(layer, hop).wait_send()
+        c, dest, copy = chunk_copy(layer)
+
+        @pl.when(dest != me)
+        def _():
+            copy.wait_send()
+
+
+def finish(scale, out_ref, gstate_ref, wgrad_ref, out_hbm, gstate_hbm, total_ref, sems):
+    copies = [
+        pltpu.make_async_copy(out_ref, out_hbm, sems.at[0]),
+        pltpu.make_async_copy(gstate_ref, gstate_hbm, sems.at[1]),
+    ]
+    for copy in copies:
+        copy.start()
+    total_ref[...] = wgrad_ref[...].astype(F32) * scale
+    for copy in copies:
+        copy.wait()
 
 
 def local_fast(n_blk, edge_state, basis, weights, partner, cotangent):
@@ -393,13 +431,13 @@
     vmem = pl.BlockSpec(memory_space=pltpu.VMEM)
     dma = pltpu.SemaphoreType.DMA
     out, gstate, wgrad = pl.pallas_call(
-        functools.partial(kernel, n_blk, 1.0 / math.sqrt(total_edges)),
+        functools.partial(kernel, n_blk),
         out_shape=(
             jax.ShapeDtypeStruct(blocks, BF16),
             jax.ShapeDtypeStruct(blocks, BF16),
-            jax.ShapeDtypeStruct((3 * CHUNK, width), F32),
+            jax.ShapeDtypeStruct((3, CHUNK, width), BF16),
         ),
-        in_specs=[pl.BlockSpec(memory_space=pl.ANY)] * 5,
+        in_specs=[pl.BlockSpec(memory_space=pltpu.HBM)] * 5,
         out_specs=(vmem, vmem, vmem),
         scratch_shapes=[
             pltpu.SMEM(partner.shape, jnp.int32),
@@ -422,7 +460,9 @@
             pltpu.VMEM((3, 2, 2, half // 8, width), BF16),
             pltpu.VMEM((3, 2, half // 8, width), BF16),
             pltpu.VMEM((3, 4, CHUNK, width), BF16),
-            pltpu.VMEM((3, 4, CHUNK, width), BF16),
+            pltpu.VMEM((3, 3, CHUNK, width), BF16),
+            pltpu.VMEM((3, CHUNK, width), BF16),
+            pltpu.VMEM((3, CHUNK, width), BF16),
             dma((7,)),
             dma((2,)),
             dma((2,)),
@@ -430,20 +470,44 @@
             dma((3,)),
             dma((3, 2, 2)),
             dma((3, 2, 2)),
-            dma((3, 4)),
-            dma((3, 4)),
+            dma((3, 3)),
+            dma((3, 3)),
+            dma((3,)),
+            dma((3,)),
         ],
         compiler_params=pltpu.CompilerParams(
-            collective_id=0, has_side_effects=True, vmem_limit_bytes=56 * 2**20
+            collective_id=0, has_side_effects=True, vmem_limit_bytes=36 * 2**20
         ),
     )(
-        partner,
-        edge_state.reshape(blocks),
-        basis.transpose(1, 2, 0),
-        weights,
-        cotangent.reshape(blocks),
-    )
-    return out.reshape(rows, width), gstate.reshape(rows, width), wgrad
+        *[
+            pltpu.with_memory_space_constraint(array, pltpu.HBM)
+            for array in (
+                partner,
+                edge_state.reshape(blocks),
+                basis.transpose(1, 2, 0),
+                weights,
+                cotangent.reshape(blocks),
+            )
+        ]
+    )
+    hbm = pl.BlockSpec(memory_space=pltpu.HBM)
+    out, gstate, wgrad = pl.pallas_call(
+        functools.partial(finish, 1.0 / math.sqrt(total_edges)),
+        out_shape=(
+            jax.ShapeDtypeStruct(blocks, BF16),
+            jax.ShapeDtypeStruct(blocks, BF16),
+            jax.ShapeDtypeStruct((3, CHUNK, width), F32),
+        ),
+        in_specs=[vmem, vmem, vmem],
+        out_specs=(hbm, hbm, vmem),
+        scratch_shapes=[dma((2,))],
+        compiler_params=pltpu.CompilerParams(vmem_limit_bytes=8 * 2**20),
+    )(out, gstate, wgrad)
+    return (
+        out.reshape(rows, width),
+        gstate.reshape(rows, width),
+        wgrad.reshape(3 * CHUNK, width),
+    )
 
 
 def norm_rows(hidden):

time: 39.3 us -> 37.8 us (0.962)
  local copies, waits for them, and re-layouts: 4.21 us -> 0 us
  Pallas kernels: 34.3 us -> 37 us
    unnamed x5 -> x0, local copies, waits for them, and re-layouts: 4.21 us -> none
    pallas_call x1 -> x2, Pallas kernels: 34.3 us -> 37 us  [the longest x1 35.5 us: local_fast(): pl.pallas_call(functools.partial(kernel, n_blk), out_shape=(jax.ShapeDtyp...]
where the time goes in v3:
time: 37.8 us; the launch traced here: 37.6 us
  Pallas kernels  37 us (98%)
  between operations  0.64 us (2%)
    pallas_call x1, Pallas kernels, local_fast(): pl.pallas_call(functools.partial(kernel, n_blk), out_shape=(jax.ShapeDtyp...  35.5 us
    pallas_call x1, Pallas kernels, local_fast(): pl.pallas_call(functools.partial(finish, 1.0 / math.sqrt(total_edges)), o...  1.53 us

profile of v3, /device:TPU:0, one launch (start us, length us, event | category | flops | bytes accessed | tf_op | source)
XLA Modules:
  0.0 37.6 jit_solution(7071054966689938743)
XLA Ops:
  0.6 35.5 %shard_map.76 = (bf16[3,128,512]{2,1,0:T(8,128)(2,1)S(1)}, bf16[3,128,512]{2,1,0:T(8,128)(2,1)S(1)}, bf16[3,16,512]{2,1,0:T(8,128)(2,1)S(1)}) custom-call(s32[3]{0:T(128)} %partner_hbm.1, bf16[3,128,512]{2,1,0:T(8,128)(2,1)} %bitcast.6, bf16[16,16,24]{2,1,0:T(8,128)(2,1)} %bitcast.8, bf16[3,512,512]{2,1,0:T(8,128)(2,1)} %w_hbm.1, bf16[3,128,512]{2,1,0:T(8,128)(2,1)} %bitcast.7), custom_call_target="tpu_custom_call" | custom-call | tf_op jit(solution)/shard_map/pallas_call | solution.py:433
  36.1 1.5 %shard_map.77 = (bf16[3,128,512]{2,1,0:T(8,128)(2,1)}, bf16[3,128,512]{2,1,0:T(8,128)(2,1)}, f32[3,16,512]{2,1,0:T(8,128)}) custom-call(bf16[3,128,512]{2,1,0:T(8,128)(2,1)S(1)} %get-tuple-element.9.out_ref, bf16[3,128,512]{2,1,0:T(8,128)(2,1)S(1)} %get-tuple-element.10.gstate_ref, bf16[3,16,512]{2,1,0:T(8,128)(2,1)S(1)} %get-tuple-element.11.wgrad_ref), custom_call_target="tpu_custom_call" | custom-call | tf_op jit(solution)/shard_map/pallas_call | solution.py:494

commit v4 on v2

--- a/solution.py
+++ b/solution.py
@@ -32,9 +32,9 @@
     return jnp.where(even, pltpu.roll(x, rows - 1, 0), pltpu.roll(x, 1, 0))
 
 
-def mixing_matrix(basis, blocks):
+def mixing_matrix(basis, block):
     flat = basis.reshape(NBR * NBR, basis.shape[2])
-    rows = BLOCK * len(blocks)
+    rows = BLOCK
 
     def iota(shape, dim):
         return lax.broadcasted_iota(jnp.int32, shape, dim)
@@ -43,11 +43,8 @@
         return hit.astype(F32).astype(BF16)
 
     atom_shape = (rows, basis.shape[2])
-    row = iota(atom_shape, 0)
-    first_atom = blocks[0] * (BLOCK // NBR)
-    if len(blocks) == 2:
-        first_atom = first_atom + (row // BLOCK) * ((blocks[1] - blocks[0]) * (BLOCK // NBR))
-    pick = mask(first_atom + (row % BLOCK) // NBR == iota(atom_shape, 1))
+    atom = block * (BLOCK // NBR) + iota(atom_shape, 0) // NBR
+    pick = mask(atom == iota(atom_shape, 1))
     own = dot(pick, flat, 1, 1)
     own_shape = (rows, NBR * NBR)
     own = jnp.where(iota(own_shape, 0) % NBR == iota(own_shape, 1) // NBR, own, 0.0).astype(BF16)
@@ -58,20 +55,23 @@
     return jnp.where(same, wide, 0.0).astype(BF16)
 
 
-def forward(h, w_ref, layer, n_ref, rows):
+def forward(h, w_ref, layer, p, saved):
+    n_ref, _, inv_ref, slope_ref = saved
     inv = inverse_rms(h)
     normed = (h * inv).astype(BF16)
-    n_ref[layer, rows, :] = normed
+    n_ref[layer, pl.ds(p * BLOCK, BLOCK), :] = normed
+    inv_ref[layer, p] = inv
     pre = dot(normed, w_ref[layer])
     s = 0.5 * jnp.tanh(0.5 * pre) + 0.5
-    slope = s * (1.0 + pre * (1.0 - s))
-    return h + pre * s, (inv, slope)
-
-
-def backward(h, saved, w_ref, layer, g, d_ref, rows):
-    inv, slope = saved
-    dpre = (g * slope).astype(BF16)
-    d_ref[layer, rows, :] = dpre
+    slope_ref[layer, p] = s * (1.0 + pre * (1.0 - s))
+    return h + pre * s
+
+
+def backward(h, w_ref, layer, p, saved, g):
+    _, d_ref, inv_ref, slope_ref = saved
+    inv = inv_ref[layer, p]
+    dpre = (g * slope_ref[layer, p]).astype(BF16)
+    d_ref[layer, pl.ds(p * BLOCK, BLOCK), :] = dpre
     dn = dot(dpre, w_ref[layer], 1, 1)
     u = h * inv
     inner = jnp.mean(dn * u, axis=-1, keepdims=True)
@@ -80,7 +80,6 @@
 
 def kernel(
     n_blk,
-    scale,
     partner_hbm,
     state_hbm,
     basis_hbm,
@@ -99,7 +98,16 @@
     eout_ref,
     gout_ref,
     sent_ref,
-    give_ref,
+    rev_ref,
+    mix_ref,
+    mixed_ref,
+    first_ref,
+    second_ref,
+    gs_ref,
+    inv_ref,
+    slope_ref,
+    pos_ref,
+    pair_ref,
     take_ref,
     half_ref,
     own_ref,
@@ -169,27 +177,21 @@
     swapped = jnp.minimum(shift * shift, 1)
     place = (1 - away0, jnp.minimum(away0 + 2 * away2, 2), 2 - 2 * away2)
 
-    def pair(ref):
-        return jnp.concatenate([ref[pos1], ref[pos2]], axis=0)
-
-    a_rows, b_rows = pl.ds(0, BLOCK), pl.ds(BLOCK, 2 * BLOCK)
+    for p, value in enumerate((first_pos, pos1, pos2)):
+        pos_ref[p] = value
+    for p, value in enumerate((0, 1 + swapped, 2 - swapped)):
+        pair_ref[p] = value
+    saved = (n_ref, d_ref, inv_ref, slope_ref)
 
     def exchange(step):
         return pltpu.make_async_remote_copy(
-            src_ref=give_ref.at[step],
+            src_ref=sent_ref.at[step, 0],
             dst_ref=take_ref.at[step],
             send_sem=give_sem.at[step],
             recv_sem=take_sem.at[step],
             device_id=(1 - x, b),
             device_id_type=MESH,
         )
-
-    def local_reverse(v, step):
-        sent_ref[step] = v.astype(BF16).reshape(2, BLOCK, width)
-        other = jnp.concatenate(
-            [sent_ref[step, swapped], sent_ref[step, 1 - swapped]], axis=0
-        )
-        return flip(other.astype(F32))
 
     def half_copy(layer):
         return pltpu.make_async_remote_copy(
@@ -280,60 +282,78 @@
             def _():
                 final_ref[c % 3, z] = piece_ref[layer, t]
 
-    loads[1].wait()
-    loads[2].wait()
-    mix_a = mixing_matrix(basis_ref[...], (first_pos,))
-    mixed_a = dot(mix_a, state_ref[first_pos])
-    loads[3].wait()
-    first_a, saved_a1 = forward(mixed_a, w_ref, 0, n_ref, a_rows)
-    loads[4].wait()
-    second_a, saved_a2 = forward(first_a, w_ref, 1, n_ref, a_rows)
-    give_ref[0] = second_a.astype(BF16)
-    pl.semaphore_wait(barrier, count - 1)
-    exchange(0).start()
-
-    mix_b = mixing_matrix(basis_ref[...], (pos1, pos2))
-    mixed_b = dot(mix_b, pair(state_ref))
-    first_b, saved_b1 = forward(mixed_b, w_ref, 0, n_ref, b_rows)
-    second_b, saved_b2 = forward(first_b, w_ref, 1, n_ref, b_rows)
-    summed_b = second_b + local_reverse(second_b, 0)
-    loads[5].wait()
-    final_b, saved_b3 = forward(summed_b, w_ref, 2, n_ref, b_rows)
-    eout_ref[pl.ds(1, 2)] = final_b.astype(BF16).reshape(2, BLOCK, width)
-
-    exchange(0).wait_recv()
-    summed_a = second_a + flip(take_ref[0].astype(F32))
-    final_a, saved_a3 = forward(summed_a, w_ref, 2, n_ref, a_rows)
-    eout_ref[0] = final_a.astype(BF16)
-    loads[6].wait()
-    gs_a = backward(
-        summed_a, saved_a3, w_ref, 2, cot_ref[first_pos].astype(F32), d_ref, a_rows
-    )
-    give_ref[1] = gs_a.astype(BF16)
-    exchange(1).start()
-
-    gs_b = backward(summed_b, saved_b3, w_ref, 2, pair(cot_ref).astype(F32), d_ref, b_rows)
+    def phase_one(p, carry):
+        mix = mixing_matrix(basis_ref[...], pos_ref[p])
+        mix_ref[p] = mix
+        mixed = dot(mix, state_ref[pos_ref[p]])
+        mixed_ref[p] = mixed
+        first = forward(mixed, w_ref, 0, p, saved)
+        first_ref[p] = first
+        second = forward(first, w_ref, 1, p, saved)
+        second_ref[p] = second
+        sent_ref[0, p] = second.astype(BF16)
+
+        @pl.when(p == 0)
+        def _():
+            pl.semaphore_wait(barrier, count - 1)
+            exchange(0).start()
+
+        return carry
+
+    def reverse(step, p):
+        @pl.when(p == 0)
+        def _():
+            exchange(step).wait_recv()
+            rev_ref[...] = take_ref[step]
+
+        @pl.when(p > 0)
+        def _():
+            rev_ref[...] = sent_ref[step, pair_ref[p]]
+
+        return flip(rev_ref[...].astype(F32))
+
+    def phase_two(i, carry):
+        p = 1 - i + 3 * (i // 2)
+        summed = second_ref[p] + reverse(0, p)
+        final = forward(summed, w_ref, 2, p, saved)
+        eout_ref[p] = final.astype(BF16)
+        g = backward(summed, w_ref, 2, p, saved, cot_ref[pos_ref[p]].astype(F32))
+        gs_ref[p] = g
+        sent_ref[1, p] = g.astype(BF16)
+
+        @pl.when(p == 0)
+        def _():
+            exchange(1).start()
+
+        return carry
+
+    def phase_three(i, carry):
+        p = (i + 1) % 3
+        g = gs_ref[p] + reverse(1, p)
+        g = backward(first_ref[p], w_ref, 1, p, saved, g)
+        g = backward(mixed_ref[p], w_ref, 0, p, saved, g)
+        gout_ref[p] = dot(mix_ref[p], g.astype(BF16), 0, 0).astype(BF16)
+
+        @pl.when(p == 2)
+        def _():
+            send_parts(2)
+
+        return carry
+
+    for load in loads[1:5]:
+        load.wait()
+    lax.fori_loop(0, 3, phase_one, 0)
+    for load in loads[5:]:
+        load.wait()
+    lax.fori_loop(0, 3, phase_two, 0)
     send_half(2)
-    gsec_b = gs_b + local_reverse(gs_b, 1)
-    gf_b = backward(first_b, saved_b2, w_ref, 1, gsec_b, d_ref, b_rows)
-    send_parts(2)
-    gm_b = backward(mixed_b, saved_b1, w_ref, 0, gf_b, d_ref, b_rows)
-    gout_ref[pl.ds(1, 2)] = dot(mix_b, gm_b.astype(BF16), 0, 0).astype(BF16).reshape(
-        2, BLOCK, width
-    )
-
-    exchange(1).wait_recv()
-    gsec_a = gs_a + flip(take_ref[1].astype(F32))
-    gf_a = backward(first_a, saved_a2, w_ref, 1, gsec_a, d_ref, a_rows)
-    send_half(1)
-    gm_a = backward(mixed_a, saved_a1, w_ref, 0, gf_a, d_ref, a_rows)
-    send_half(0)
+    lax.fori_loop(0, 3, phase_three, 0)
+    lax.fori_loop(0, 2, lambda i, carry: (send_half(1 - i), carry)[1], 0)
+    send_quads(2)
     send_parts(1)
-    send_quads(2)
     send_parts(0)
-    gout_ref[0] = dot(mix_a, gm_a.astype(BF16), 0, 0).astype(BF16)
+    send_pieces(2)
     send_quads(1)
-    send_pieces(2)
     send_quads(0)
 
     for k in range(3):
@@ -368,7 +388,7 @@
         total = final_ref[j, 0].astype(F32)
         for plane in range(1, 4):
             total = total + final_ref[j, plane].astype(F32)
-        wgrad_ref[pl.ds(j * CHUNK, CHUNK), :] = total * scale
+        wgrad_ref[j] = total
 
     for step in range(2):
         exchange(step).wait_send()
@@ -385,6 +405,18 @@
                 copy.wait_send()
 
 
+def finish(scale, out_ref, gstate_ref, wgrad_ref, out_hbm, gstate_hbm, total_ref, sems):
+    copies = [
+        pltpu.make_async_copy(out_ref, out_hbm, sems.at[0]),
+        pltpu.make_async_copy(gstate_ref, gstate_hbm, sems.at[1]),
+    ]
+    for copy in copies:
+        copy.start()
+    total_ref[...] = wgrad_ref[...] * scale
+    for copy in copies:
+        copy.wait()
+
+
 def local_fast(n_blk, edge_state, basis, weights, partner, cotangent):
     rows, width = edge_state.shape
     total_edges = rows * 2 * n_blk
@@ -393,13 +425,13 @@
     vmem = pl.BlockSpec(memory_space=pltpu.VMEM)
     dma = pltpu.SemaphoreType.DMA
     out, gstate, wgrad = pl.pallas_call(
-        functools.partial(kernel, n_blk, 1.0 / math.sqrt(total_edges)),
+        functools.partial(kernel, n_blk),
         out_shape=(
             jax.ShapeDtypeStruct(blocks, BF16),
             jax.ShapeDtypeStruct(blocks, BF16),
-            jax.ShapeDtypeStruct((3 * CHUNK, width), F32),
+            jax.ShapeDtypeStruct((3, CHUNK, width), F32),
         ),
-        in_specs=[pl.BlockSpec(memory_space=pl.ANY)] * 5,
+        in_specs=[pl.BlockSpec(memory_space=pltpu.HBM)] * 5,
         out_specs=(vmem, vmem, vmem),
         scratch_shapes=[
             pltpu.SMEM(partner.shape, jnp.int32),
@@ -411,8 +443,17 @@
             pltpu.VMEM((3, rows, width), BF16),
             pltpu.VMEM(blocks, BF16),
             pltpu.VMEM(blocks, BF16),
-            pltpu.VMEM((2, 2, BLOCK, width), BF16),
-            pltpu.VMEM((2, BLOCK, width), BF16),
+            pltpu.VMEM((2, 3, BLOCK, width), BF16),
+            pltpu.VMEM((BLOCK, width), BF16),
+            pltpu.VMEM((3, BLOCK, BLOCK), BF16),
+            pltpu.VMEM(blocks, F32),
+            pltpu.VMEM(blocks, F32),
+            pltpu.VMEM(blocks, F32),
+            pltpu.VMEM(blocks, F32),
+            pltpu.VMEM((3, 3, BLOCK, 1), F32),
+            pltpu.VMEM((3, 3, BLOCK, width), F32),
+            pltpu.SMEM((3,), jnp.int32),
+            pltpu.SMEM((3,), jnp.int32),
             pltpu.VMEM((2, BLOCK, width), BF16),
             pltpu.VMEM((3, half, width), BF16),
             pltpu.VMEM((3, half, width), F32),
@@ -434,16 +475,38 @@
             dma((3, 4)),
         ],
         compiler_params=pltpu.CompilerParams(
-            collective_id=0, has_side_effects=True, vmem_limit_bytes=56 * 2**20
+            collective_id=0, has_side_effects=True, vmem_limit_bytes=36 * 2**20
         ),
     )(
-        partner,
-        edge_state.reshape(blocks),
-        basis.transpose(1, 2, 0),
-        weights,
-        cotangent.reshape(blocks),
-    )
-    return out.reshape(rows, width), gstate.reshape(rows, width), wgrad
+        *[
+            pltpu.with_memory_space_constraint(array, pltpu.HBM)
+            for array in (
+                partner,
+                edge_state.reshape(blocks),
+                basis.transpose(1, 2, 0),
+                weights,
+                cotangent.reshape(blocks),
+            )
+        ]
+    )
+    hbm = pl.BlockSpec(memory_space=pltpu.HBM)
+    out, gstate, wgrad = pl.pallas_call(
+        functools.partial(finish, 1.0 / math.sqrt(total_edges)),
+        out_shape=(
+            jax.ShapeDtypeStruct(blocks, BF16),
+            jax.ShapeDtypeStruct(blocks, BF16),
+            jax.ShapeDtypeStruct((3, CHUNK, width), F32),
+        ),
+        in_specs=[vmem, vmem, vmem],
+        out_specs=(hbm, hbm, vmem),
+        scratch_shapes=[dma((2,))],
+        compiler_params=pltpu.CompilerParams(vmem_limit_bytes=8 * 2**20),
+    )(out, gstate, wgrad)
+    return (
+        out.reshape(rows, width),
+        gstate.reshape(rows, width),
+        wgrad.reshape(3 * CHUNK, width),
+    )
 
 
 def norm_rows(hidden):

time: 39.3 us -> 37.1 us (0.944)
  local copies, waits for them, and re-layouts: 4.21 us -> 0 us
  Pallas kernels: 34.3 us -> 36.3 us
    unnamed x5 -> x0, local copies, waits for them, and re-layouts: 4.21 us -> none
    pallas_call x1 -> x2, Pallas kernels: 34.3 us -> 36.3 us  [the longest x1 34.8 us: local_fast(): pl.pallas_call(functools.partial(kernel, n_blk), out_shape=(jax.ShapeDtyp...]
where the time goes in v4:
time: 37.1 us; the launch traced here: 36.9 us
  Pallas kernels  36.3 us (98%)
  between operations  0.64 us (2%)
    pallas_call x1, Pallas kernels, local_fast(): pl.pallas_call(functools.partial(kernel, n_blk), out_shape=(jax.ShapeDtyp...  34.8 us
    pallas_call x1, Pallas kernels, local_fast(): pl.pallas_call(functools.partial(finish, 1.0 / math.sqrt(total_edges)), o...  1.53 us

profile of v4, /device:TPU:0, one launch (start us, length us, event | category | flops | bytes accessed | tf_op | source)
XLA Modules:
  0.0 36.9 jit_solution(13031584701243165324)
XLA Ops:
  0.6 34.8 %shard_map.76 = (bf16[3,128,512]{2,1,0:T(8,128)(2,1)S(1)}, bf16[3,128,512]{2,1,0:T(8,128)(2,1)S(1)}, f32[3,16,512]{2,1,0:T(8,128)S(1)}) custom-call(s32[3]{0:T(128)} %partner_hbm.1, bf16[3,128,512]{2,1,0:T(8,128)(2,1)} %bitcast.6, bf16[16,16,24]{2,1,0:T(8,128)(2,1)} %bitcast.8, bf16[3,512,512]{2,1,0:T(8,128)(2,1)} %w_hbm.1, bf16[3,128,512]{2,1,0:T(8,128)(2,1)} %bitcast.7), custom_call_target="tpu_custom_call" | custom-call | tf_op jit(solution)/shard_map/pallas_call | solution.py:427
  35.4 1.5 %shard_map.77 = (bf16[3,128,512]{2,1,0:T(8,128)(2,1)}, bf16[3,128,512]{2,1,0:T(8,128)(2,1)}, f32[3,16,512]{2,1,0:T(8,128)}) custom-call(bf16[3,128,512]{2,1,0:T(8,128)(2,1)S(1)} %get-tuple-element.9.out_ref, bf16[3,128,512]{2,1,0:T(8,128)(2,1)S(1)} %get-tuple-element.10.gstate_ref, f32[3,16,512]{2,1,0:T(8,128)S(1)} %get-tuple-element.11.wgrad_ref), custom_call_target="tpu_custom_call" | custom-call | tf_op jit(solution)/shard_map/pallas_call | solution.py:493

commit v5 on v4

--- a/solution.py
+++ b/solution.py
@@ -114,6 +114,7 @@
     half_in_ref,
     part_ref,
     part_in_ref,
+    direct_in_ref,
     quad_ref,
     quad_in_ref,
     piece_ref,
@@ -125,6 +126,8 @@
     half_in_sem,
     part_sem,
     part_in_sem,
+    direct_sem,
+    direct_in_sem,
     piece_sem,
     final_sem,
 ):
@@ -215,11 +218,23 @@
         half_copy(layer).start()
         own_ref[layer] = dot(columns(core), d, 0, 0)
 
+    def direct_copy(r):
+        px = 1 - x if r >= 2 else x
+        py = 1 - y if r % 2 else y
+        return pltpu.make_async_remote_copy(
+            src_ref=part_ref.at[0, px, py],
+            dst_ref=direct_in_ref.at[r - 1],
+            send_sem=direct_sem.at[r - 1],
+            recv_sem=direct_in_sem.at[r - 1],
+            device_id=(px, 4 * z + 2 * py + core),
+            device_id_type=MESH,
+        )
+
     def sides(layer, piece):
-        return (x, y) if piece == 1 and layer < 2 else (y, x)
+        return (x, y) if piece == 1 and layer == 1 else (y, x)
 
     def part_copy(layer, piece, hop):
-        along_x = (piece == 1 and layer < 2) == (hop == 0)
+        along_x = (piece == 1 and layer == 1) == (hop == 0)
         near, far = sides(layer, piece)
         if hop == 0:
             src, dst = part_ref.at[layer, piece, 1 - near], part_in_ref.at[layer, piece]
@@ -238,8 +253,12 @@
         half_copy(layer).wait_recv()
         total = own_ref[layer] + half_in_ref[layer].astype(F32)
         part_ref[layer] = total.astype(BF16).reshape(2, 2, 2, eighth, width)
-        for piece in range(2):
-            part_copy(layer, piece, 0).start()
+        if layer == 0:
+            for r in (3, 2, 1):
+                direct_copy(r).start()
+        else:
+            for piece in range(2):
+                part_copy(layer, piece, 0).start()
 
     def send_quads(layer):
         for piece in range(2):
@@ -252,7 +271,10 @@
 
     def piece_copy(layer, t):
         near, far = sides(layer, t // 2)
-        c = 32 * layer + 16 * core + 8 * (t // 2) + 4 * near + 2 * far + t % 2
+        if layer == 0:
+            c = 16 * core + 8 * x + 4 * y + t
+        else:
+            c = 32 * layer + 16 * core + 8 * (t // 2) + 4 * near + 2 * far + t % 2
         dest = c // 3
         copy = pltpu.make_async_remote_copy(
             src_ref=piece_ref.at[layer, t],
@@ -265,12 +287,21 @@
         return c, dest, copy
 
     def send_pieces(layer):
-        for piece in range(2):
-            part_copy(layer, piece, 1).wait_recv()
-            _, far = sides(layer, piece)
-            total = quad_ref[layer, piece, far].astype(F32)
-            total = total + quad_in_ref[layer, piece].astype(F32)
-            piece_ref[layer, pl.ds(2 * piece, 2)] = total.astype(BF16).reshape(2, CHUNK, width)
+        if layer == 0:
+            total = part_ref[0, x, y].astype(F32)
+            for r in (1, 2, 3):
+                direct_copy(r).wait_recv()
+                total = total + direct_in_ref[r - 1].astype(F32)
+            piece_ref[0] = total.astype(BF16).reshape(4, CHUNK, width)
+        else:
+            for piece in range(2):
+                part_copy(layer, piece, 1).wait_recv()
+                _, far = sides(layer, piece)
+                total = quad_ref[layer, piece, far].astype(F32)
+                total = total + quad_in_ref[layer, piece].astype(F32)
+                piece_ref[layer, pl.ds(2 * piece, 2)] = total.astype(BF16).reshape(
+                    2, CHUNK, width
+                )
         for t in range(4):
             c, dest, copy = piece_copy(layer, t)
 
@@ -348,28 +379,28 @@
     lax.fori_loop(0, 3, phase_two, 0)
     send_half(2)
     lax.fori_loop(0, 3, phase_three, 0)
-    lax.fori_loop(0, 2, lambda i, carry: (send_half(1 - i), carry)[1], 0)
+    lax.fori_loop(0, 2, lambda i, carry: (send_half(i), carry)[1], 0)
+    send_parts(0)
     send_quads(2)
     send_parts(1)
-    send_parts(0)
     send_pieces(2)
+    send_pieces(0)
     send_quads(1)
-    send_quads(0)
 
     for k in range(3):
         out_ref[k] = eout_ref[place[k]]
         gstate_ref[k] = gout_ref[place[k]]
 
     send_pieces(1)
-    send_pieces(0)
 
     for j in range(3):
         c = 3 * me + j
         i = c % 32
         near, far = (i // 4) % 2, (i // 2) % 2
-        x_first = ((i // 8) % 2) * (1 - c // 64)
+        layer = c // 32
+        x_first = ((i // 8) % 2) * (layer % 2)
         from_y = near + x_first * (far - near)
-        from_x = far + x_first * (near - far)
+        from_x = far + x_first * (near - far) + ((2 - layer) // 2) * ((i // 8) % 2 - far)
         for plane in range(4):
             source = from_x * n_blk + 4 * plane + 2 * from_y + i // 16
 
@@ -394,9 +425,13 @@
         exchange(step).wait_send()
     for layer in range(3):
         half_copy(layer).wait_send()
-        for piece in range(2):
-            for hop in range(2):
-                part_copy(layer, piece, hop).wait_send()
+        if layer == 0:
+            for r in (1, 2, 3):
+                direct_copy(r).wait_send()
+        else:
+            for piece in range(2):
+                for hop in range(2):
+                    part_copy(layer, piece, hop).wait_send()
         for t in range(4):
             c, dest, copy = piece_copy(layer, t)
 
@@ -460,6 +495,7 @@
             pltpu.VMEM((3, half, width), BF16),
             pltpu.VMEM((3, 2, 2, 2, half // 8, width), BF16),
             pltpu.VMEM((3, 2, 2, half // 8, width), BF16),
+            pltpu.VMEM((3, 2, half // 8, width), BF16),
             pltpu.VMEM((3, 2, 2, half // 8, width), BF16),
             pltpu.VMEM((3, 2, half // 8, width), BF16),
             pltpu.VMEM((3, 4, CHUNK, width), BF16),
@@ -471,6 +507,8 @@
             dma((3,)),
             dma((3, 2, 2)),
             dma((3, 2, 2)),
+            dma((3,)),
+            dma((3,)),
             dma((3, 4)),
             dma((3, 4)),
         ],

time: 37.1 us -> 36.7 us (0.989)
  Pallas kernels: 36.3 us -> 35.9 us
where the time goes in v5:
time: 36.7 us; the launch traced here: 36.6 us
  Pallas kernels  35.9 us (98%)
  between operations  0.64 us (2%)
    pallas_call x1, Pallas kernels, local_fast(): pl.pallas_call(functools.partial(kernel, n_blk), out_shape=(jax.ShapeDtyp...  34.4 us
    pallas_call x1, Pallas kernels, local_fast(): pl.pallas_call(functools.partial(finish, 1.0 / math.sqrt(total_edges)), o...  1.53 us

profile of v5, /device:TPU:0, one launch (start us, length us, event | category | flops | bytes accessed | tf_op | source)
XLA Modules:
  0.0 36.6 jit_solution(11506358337612635086)
XLA Ops:
  0.6 34.4 %shard_map.76 = (bf16[3,128,512]{2,1,0:T(8,128)(2,1)S(1)}, bf16[3,128,512]{2,1,0:T(8,128)(2,1)S(1)}, f32[3,16,512]{2,1,0:T(8,128)S(1)}) custom-call(s32[3]{0:T(128)} %partner_hbm.1, bf16[3,128,512]{2,1,0:T(8,128)(2,1)} %bitcast.6, bf16[16,16,24]{2,1,0:T(8,128)(2,1)} %bitcast.8, bf16[3,512,512]{2,1,0:T(8,128)(2,1)} %w_hbm.1, bf16[3,128,512]{2,1,0:T(8,128)(2,1)} %bitcast.7), custom_call_target="tpu_custom_call" | custom-call | tf_op jit(solution)/shard_map/pallas_call | solution.py:462
  35.1 1.5 %shard_map.77 = (bf16[3,128,512]{2,1,0:T(8,128)(2,1)}, bf16[3,128,512]{2,1,0:T(8,128)(2,1)}, f32[3,16,512]{2,1,0:T(8,128)}) custom-call(bf16[3,128,512]{2,1,0:T(8,128)(2,1)S(1)} %get-tuple-element.9.out_ref, bf16[3,128,512]{2,1,0:T(8,128)(2,1)S(1)} %get-tuple-element.10.gstate_ref, f32[3,16,512]{2,1,0:T(8,128)S(1)} %get-tuple-element.11.wgrad_ref), custom_call_target="tpu_custom_call" | custom-call | tf_op jit(solution)/shard_map/pallas_call | solution.py:531

commit v6 on v5

--- a/solution.py
+++ b/solution.py
@@ -99,6 +99,7 @@
     gout_ref,
     sent_ref,
     rev_ref,
+    gm_ref,
     mix_ref,
     mixed_ref,
     first_ref,
@@ -218,24 +219,21 @@
         half_copy(layer).start()
         own_ref[layer] = dot(columns(core), d, 0, 0)
 
-    def direct_copy(r):
+    def direct_copy(layer, r):
         px = 1 - x if r >= 2 else x
         py = 1 - y if r % 2 else y
         return pltpu.make_async_remote_copy(
-            src_ref=part_ref.at[0, px, py],
-            dst_ref=direct_in_ref.at[r - 1],
-            send_sem=direct_sem.at[r - 1],
-            recv_sem=direct_in_sem.at[r - 1],
+            src_ref=part_ref.at[layer, px, py],
+            dst_ref=direct_in_ref.at[layer, r - 1],
+            send_sem=direct_sem.at[layer, r - 1],
+            recv_sem=direct_in_sem.at[layer, r - 1],
             device_id=(px, 4 * z + 2 * py + core),
             device_id_type=MESH,
         )
 
-    def sides(layer, piece):
-        return (x, y) if piece == 1 and layer == 1 else (y, x)
-
     def part_copy(layer, piece, hop):
-        along_x = (piece == 1 and layer == 1) == (hop == 0)
-        near, far = sides(layer, piece)
+        along_x = hop == 1
+        near, far = y, x
         if hop == 0:
             src, dst = part_ref.at[layer, piece, 1 - near], part_in_ref.at[layer, piece]
         else:
@@ -253,9 +251,9 @@
         half_copy(layer).wait_recv()
         total = own_ref[layer] + half_in_ref[layer].astype(F32)
         part_ref[layer] = total.astype(BF16).reshape(2, 2, 2, eighth, width)
-        if layer == 0:
+        if layer < 2:
             for r in (3, 2, 1):
-                direct_copy(r).start()
+                direct_copy(layer, r).start()
         else:
             for piece in range(2):
                 part_copy(layer, piece, 0).start()
@@ -263,18 +261,16 @@
     def send_quads(layer):
         for piece in range(2):
             part_copy(layer, piece, 0).wait_recv()
-            near, _ = sides(layer, piece)
-            total = part_ref[layer, piece, near].astype(F32)
+            total = part_ref[layer, piece, y].astype(F32)
             total = total + part_in_ref[layer, piece].astype(F32)
             quad_ref[layer, piece] = total.astype(BF16)
             part_copy(layer, piece, 1).start()
 
     def piece_copy(layer, t):
-        near, far = sides(layer, t // 2)
-        if layer == 0:
-            c = 16 * core + 8 * x + 4 * y + t
+        if layer < 2:
+            c = 32 * layer + 16 * core + 8 * x + 4 * y + t
         else:
-            c = 32 * layer + 16 * core + 8 * (t // 2) + 4 * near + 2 * far + t % 2
+            c = 32 * layer + 16 * core + 8 * (t // 2) + 4 * y + 2 * x + t % 2
         dest = c // 3
         copy = pltpu.make_async_remote_copy(
             src_ref=piece_ref.at[layer, t],
@@ -287,17 +283,16 @@
         return c, dest, copy
 
     def send_pieces(layer):
-        if layer == 0:
-            total = part_ref[0, x, y].astype(F32)
+        if layer < 2:
+            total = part_ref[layer, x, y].astype(F32)
             for r in (1, 2, 3):
-                direct_copy(r).wait_recv()
-                total = total + direct_in_ref[r - 1].astype(F32)
-            piece_ref[0] = total.astype(BF16).reshape(4, CHUNK, width)
+                direct_copy(layer, r).wait_recv()
+                total = total + direct_in_ref[layer, r - 1].astype(F32)
+            piece_ref[layer] = total.astype(BF16).reshape(4, CHUNK, width)
         else:
             for piece in range(2):
                 part_copy(layer, piece, 1).wait_recv()
-                _, far = sides(layer, piece)
-                total = quad_ref[layer, piece, far].astype(F32)
+                total = quad_ref[layer, piece, x].astype(F32)
                 total = total + quad_in_ref[layer, piece].astype(F32)
                 piece_ref[layer, pl.ds(2 * piece, 2)] = total.astype(BF16).reshape(
                     2, CHUNK, width
@@ -363,7 +358,11 @@
         g = gs_ref[p] + reverse(1, p)
         g = backward(first_ref[p], w_ref, 1, p, saved, g)
         g = backward(mixed_ref[p], w_ref, 0, p, saved, g)
-        gout_ref[p] = dot(mix_ref[p], g.astype(BF16), 0, 0).astype(BF16)
+        gm_ref[...] = g.astype(BF16)
+
+        @pl.when(p > 0)
+        def _():
+            gout_ref[p] = dot(mix_ref[p], gm_ref[...], 0, 0).astype(BF16)
 
         @pl.when(p == 2)
         def _():
@@ -383,9 +382,9 @@
     send_parts(0)
     send_quads(2)
     send_parts(1)
+    gout_ref[0] = dot(mix_ref[0], gm_ref[...], 0, 0).astype(BF16)
     send_pieces(2)
     send_pieces(0)
-    send_quads(1)
 
     for k in range(3):
         out_ref[k] = eout_ref[place[k]]
@@ -396,11 +395,8 @@
     for j in range(3):
         c = 3 * me + j
         i = c % 32
-        near, far = (i // 4) % 2, (i // 2) % 2
-        layer = c // 32
-        x_first = ((i // 8) % 2) * (layer % 2)
-        from_y = near + x_first * (far - near)
-        from_x = far + x_first * (near - far) + ((2 - layer) // 2) * ((i // 8) % 2 - far)
+        from_y = (i // 4) % 2
+        from_x = (i // 8) % 2 + (c // 64) * ((i // 2) % 2 - (i // 8) % 2)
         for plane in range(4):
             source = from_x * n_blk + 4 * plane + 2 * from_y + i // 16
 
@@ -425,9 +421,9 @@
         exchange(step).wait_send()
     for layer in range(3):
         half_copy(layer).wait_send()
-        if layer == 0:
+        if layer < 2:
             for r in (1, 2, 3):
-                direct_copy(r).wait_send()
+                direct_copy(layer, r).wait_send()
         else:
             for piece in range(2):
                 for hop in range(2):
@@ -440,14 +436,18 @@
                 copy.wait_send()
 
 
-def finish(scale, out_ref, gstate_ref, wgrad_ref, out_hbm, gstate_hbm, total_ref, sems):
+def finish(
+    scale, out_ref, gstate_ref, wgrad_ref, out_hbm, gstate_hbm, total_hbm, total_ref, sems
+):
     copies = [
         pltpu.make_async_copy(out_ref, out_hbm, sems.at[0]),
         pltpu.make_async_copy(gstate_ref, gstate_hbm, sems.at[1]),
+        pltpu.make_async_copy(total_ref, total_hbm, sems.at[2]),
     ]
-    for copy in copies:
-        copy.start()
+    copies[0].start()
+    copies[1].start()
     total_ref[...] = wgrad_ref[...] * scale
+    copies[2].start()
     for copy in copies:
         copy.wait()
 
@@ -480,6 +480,7 @@
             pltpu.VMEM(blocks, BF16),
             pltpu.VMEM((2, 3, BLOCK, width), BF16),
             pltpu.VMEM((BLOCK, width), BF16),
+            pltpu.VMEM((BLOCK, width), BF16),
             pltpu.VMEM((3, BLOCK, BLOCK), BF16),
             pltpu.VMEM(blocks, F32),
             pltpu.VMEM(blocks, F32),
@@ -495,7 +496,7 @@
             pltpu.VMEM((3, half, width), BF16),
             pltpu.VMEM((3, 2, 2, 2, half // 8, width), BF16),
             pltpu.VMEM((3, 2, 2, half // 8, width), BF16),
-            pltpu.VMEM((3, 2, half // 8, width), BF16),
+            pltpu.VMEM((2, 3, 2, half // 8, width), BF16),
             pltpu.VMEM((3, 2, 2, half // 8, width), BF16),
             pltpu.VMEM((3, 2, half // 8, width), BF16),
             pltpu.VMEM((3, 4, CHUNK, width), BF16),
@@ -507,8 +508,8 @@
             dma((3,)),
             dma((3, 2, 2)),
             dma((3, 2, 2)),
-            dma((3,)),
-            dma((3,)),
+            dma((2, 3)),
+            dma((2, 3)),
             dma((3, 4)),
             dma((3, 4)),
         ],
@@ -536,8 +537,8 @@
             jax.ShapeDtypeStruct((3, CHUNK, width), F32),
         ),
         in_specs=[vmem, vmem, vmem],
-        out_specs=(hbm, hbm, vmem),
-        scratch_shapes=[dma((2,))],
+        out_specs=(hbm, hbm, hbm),
+        scratch_shapes=[pltpu.VMEM((3, CHUNK, width), F32), dma((3,))],
         compiler_params=pltpu.CompilerParams(vmem_limit_bytes=8 * 2**20),
     )(out, gstate, wgrad)
     return (

time: 36.7 us -> 34.2 us (0.932)
  Pallas kernels: 35.9 us -> 33.4 us
    pallas_call x1, Pallas kernels: 34.4 us -> 32.5 us  [local_fast(): pl.pallas_call(functools.partial(kernel, n_blk), out_shape=(jax.ShapeDtyp...]
    pallas_call x1, Pallas kernels: 1.53 us -> 0.93 us  [local_fast(): pl.pallas_call(functools.partial(finish, 1.0 / math.sqrt(total_edges)), o...]
where the time goes in v6:
time: 34.2 us; the launch traced here: 34.1 us
  Pallas kernels  33.4 us (98%)
  between operations  0.64 us (2%)
    pallas_call x1, Pallas kernels, local_fast(): pl.pallas_call(functools.partial(kernel, n_blk), out_shape=(jax.ShapeDtyp...  32.5 us
    pallas_call x1, Pallas kernels, local_fast(): pl.pallas_call(functools.partial(finish, 1.0 / math.sqrt(total_edges)), o...  0.93 us

profile of v6, /device:TPU:0, one launch (start us, length us, event | category | flops | bytes accessed | tf_op | source)
XLA Modules:
  0.0 34.1 jit_solution(8494328813382092241)
XLA Ops:
  0.6 32.5 %shard_map.76 = (bf16[3,128,512]{2,1,0:T(8,128)(2,1)S(1)}, bf16[3,128,512]{2,1,0:T(8,128)(2,1)S(1)}, f32[3,16,512]{2,1,0:T(8,128)S(1)}) custom-call(s32[3]{0:T(128)} %partner_hbm.1, bf16[3,128,512]{2,1,0:T(8,128)(2,1)} %bitcast.6, bf16[16,16,24]{2,1,0:T(8,128)(2,1)} %bitcast.8, bf16[3,512,512]{2,1,0:T(8,128)(2,1)} %w_hbm.1, bf16[3,128,512]{2,1,0:T(8,128)(2,1)} %bitcast.7), custom_call_target="tpu_custom_call" | custom-call | tf_op jit(solution)/shard_map/pallas_call | solution.py:462
  33.1 0.9 %shard_map.77 = (bf16[3,128,512]{2,1,0:T(8,128)(2,1)}, bf16[3,128,512]{2,1,0:T(8,128)(2,1)}, f32[3,16,512]{2,1,0:T(8,128)}) custom-call(bf16[3,128,512]{2,1,0:T(8,128)(2,1)S(1)} %get-tuple-element.9.out_ref, bf16[3,128,512]{2,1,0:T(8,128)(2,1)S(1)} %get-tuple-element.10.gstate_ref, f32[3,16,512]{2,1,0:T(8,128)S(1)} %get-tuple-element.11.wgrad_ref), custom_call_target="tpu_custom_call" | custom-call | tf_op jit(solution)/shard_map/pallas_call | solution.py:532

commit v7 on v6

--- a/solution.py
+++ b/solution.py
@@ -383,13 +383,13 @@
     send_quads(2)
     send_parts(1)
     gout_ref[0] = dot(mix_ref[0], gm_ref[...], 0, 0).astype(BF16)
-    send_pieces(2)
-    send_pieces(0)
 
     for k in range(3):
         out_ref[k] = eout_ref[place[k]]
         gstate_ref[k] = gout_ref[place[k]]
 
+    send_pieces(0)
+    send_pieces(2)
     send_pieces(1)
 
     for j in range(3):

time: 34.2 us -> 34.9 us (1.020)
  Pallas kernels: 33.4 us -> 34.1 us
    pallas_call x1, Pallas kernels: 32.5 us -> 33.2 us  [local_fast(): pl.pallas_call(functools.partial(kernel, n_blk), out_shape=(jax.ShapeDtyp...]
where the time goes in v7:
time: 34.9 us; the launch traced here: 34.7 us
  Pallas kernels  34.1 us (98%)
  between operations  0.64 us (2%)
    pallas_call x1, Pallas kernels, local_fast(): pl.pallas_call(functools.partial(kernel, n_blk), out_shape=(jax.ShapeDtyp...  33.2 us
    pallas_call x1, Pallas kernels, local_fast(): pl.pallas_call(functools.partial(finish, 1.0 / math.sqrt(total_edges)), o...  0.93 us

profile of v7, /device:TPU:0, one launch (start us, length us, event | category | flops | bytes accessed | tf_op | source)
XLA Modules:
  0.0 34.7 jit_solution(17846496594505441151)
XLA Ops:
  0.6 33.2 %shard_map.76 = (bf16[3,128,512]{2,1,0:T(8,128)(2,1)S(1)}, bf16[3,128,512]{2,1,0:T(8,128)(2,1)S(1)}, f32[3,16,512]{2,1,0:T(8,128)S(1)}) custom-call(s32[3]{0:T(128)} %partner_hbm.1, bf16[3,128,512]{2,1,0:T(8,128)(2,1)} %bitcast.6, bf16[16,16,24]{2,1,0:T(8,128)(2,1)} %bitcast.8, bf16[3,512,512]{2,1,0:T(8,128)(2,1)} %w_hbm.1, bf16[3,128,512]{2,1,0:T(8,128)(2,1)} %bitcast.7), custom_call_target="tpu_custom_call" | custom-call | tf_op jit(solution)/shard_map/pallas_call | solution.py:462
  33.8 0.9 %shard_map.77 = (bf16[3,128,512]{2,1,0:T(8,128)(2,1)}, bf16[3,128,512]{2,1,0:T(8,128)(2,1)}, f32[3,16,512]{2,1,0:T(8,128)}) custom-call(bf16[3,128,512]{2,1,0:T(8,128)(2,1)S(1)} %get-tuple-element.9.out_ref, bf16[3,128,512]{2,1,0:T(8,128)(2,1)S(1)} %get-tuple-element.10.gstate_ref, f32[3,16,512]{2,1,0:T(8,128)S(1)} %get-tuple-element.11.wgrad_ref), custom_call_target="tpu_custom_call" | custom-call | tf_op jit(solution)/shard_map/pallas_call | solution.py:532

commit v8 on v6

--- a/solution.py
+++ b/solution.py
@@ -219,11 +219,16 @@
         half_copy(layer).start()
         own_ref[layer] = dot(columns(core), d, 0, 0)
 
+    def row_group(layer, px, py, pc):
+        first, second = (2 - layer) // 2, layer % 2
+        turn = first * px * (1 - pc) + second * (1 - (px - pc) * (px - pc))
+        return py + turn * (1 - 2 * py)
+
     def direct_copy(layer, r):
         px = 1 - x if r >= 2 else x
         py = 1 - y if r % 2 else y
         return pltpu.make_async_remote_copy(
-            src_ref=part_ref.at[layer, px, py],
+            src_ref=part_ref.at[layer, px, row_group(layer, px, py, core)],
             dst_ref=direct_in_ref.at[layer, r - 1],
             send_sem=direct_sem.at[layer, r - 1],
             recv_sem=direct_in_sem.at[layer, r - 1],
@@ -268,7 +273,7 @@
 
     def piece_copy(layer, t):
         if layer < 2:
-            c = 32 * layer + 16 * core + 8 * x + 4 * y + t
+            c = 32 * layer + 16 * core + 8 * x + 4 * row_group(layer, x, y, core) + t
         else:
             c = 32 * layer + 16 * core + 8 * (t // 2) + 4 * y + 2 * x + t % 2
         dest = c // 3
@@ -284,7 +289,7 @@
 
     def send_pieces(layer):
         if layer < 2:
-            total = part_ref[layer, x, y].astype(F32)
+            total = part_ref[layer, x, row_group(layer, x, y, core)].astype(F32)
             for r in (1, 2, 3):
                 direct_copy(layer, r).wait_recv()
                 total = total + direct_in_ref[layer, r - 1].astype(F32)
@@ -395,7 +400,7 @@
     for j in range(3):
         c = 3 * me + j
         i = c % 32
-        from_y = (i // 4) % 2
+        from_y = row_group(c // 32, (i // 8) % 2, (i // 4) % 2, i // 16)
         from_x = (i // 8) % 2 + (c // 64) * ((i // 2) % 2 - (i // 8) % 2)
         for plane in range(4):
             source = from_x * n_blk + 4 * plane + 2 * from_y + i // 16

time: 34.2 us -> 34.2 us (level)
  no operation moved by 1% of the time
where the time goes in v8:
time: 34.2 us; the launch traced here: 34.1 us
  Pallas kernels  33.4 us (98%)
  between operations  0.64 us (2%)
    pallas_call x1, Pallas kernels, local_fast(): pl.pallas_call(functools.partial(kernel, n_blk), out_shape=(jax.ShapeDtyp...  32.5 us
    pallas_call x1, Pallas kernels, local_fast(): pl.pallas_call(functools.partial(finish, 1.0 / math.sqrt(total_edges)), o...  0.93 us

profile of v8, /device:TPU:0, one launch (start us, length us, event | category | flops | bytes accessed | tf_op | source)
XLA Modules:
  0.0 34.1 jit_solution(11402621271448716324)
XLA Ops:
  0.6 32.5 %shard_map.76 = (bf16[3,128,512]{2,1,0:T(8,128)(2,1)S(1)}, bf16[3,128,512]{2,1,0:T(8,128)(2,1)S(1)}, f32[3,16,512]{2,1,0:T(8,128)S(1)}) custom-call(s32[3]{0:T(128)} %partner_hbm.1, bf16[3,128,512]{2,1,0:T(8,128)(2,1)} %bitcast.6, bf16[16,16,24]{2,1,0:T(8,128)(2,1)} %bitcast.8, bf16[3,512,512]{2,1,0:T(8,128)(2,1)} %w_hbm.1, bf16[3,128,512]{2,1,0:T(8,128)(2,1)} %bitcast.7), custom_call_target="tpu_custom_call" | custom-call | tf_op jit(solution)/shard_map/pallas_call | solution.py:467
  33.2 0.9 %shard_map.77 = (bf16[3,128,512]{2,1,0:T(8,128)(2,1)}, bf16[3,128,512]{2,1,0:T(8,128)(2,1)}, f32[3,16,512]{2,1,0:T(8,128)}) custom-call(bf16[3,128,512]{2,1,0:T(8,128)(2,1)S(1)} %get-tuple-element.9.out_ref, bf16[3,128,512]{2,1,0:T(8,128)(2,1)S(1)} %get-tuple-element.10.gstate_ref, f32[3,16,512]{2,1,0:T(8,128)S(1)} %get-tuple-element.11.wgrad_ref), custom_call_target="tpu_custom_call" | custom-call | tf_op jit(solution)/shard_map/pallas_call | solution.py:537
